TPU v7x, 256 devices: a whole 4x4x8 slice. The times are simulated.
256 devices in a mesh: ctx: 4 (over x_lo, core), vocab: 64 (over z, y, x_hi).
Axes of the slice: x: 4 (x_hi: 2, x_lo: 2; x = x_hi * 2 + x_lo), y: 4, z: 8, core: 2. Of those that a mesh axis runs over, the one named last changes fastest.
Arguments:
- hidden: bfloat16 [256, 2, 5120], P('ctx'), may hold values from -6 to 6
- gain: bfloat16 [5120], replicated, may hold values from 0.5 to 1.5
- head: bfloat16 [5120, 81920], P('ctx', 'vocab'), as said below
- targets: int32 [256, 2], P('ctx'), may hold values from 0 to 81919
- prompt_length: int32 [2], replicated, may hold values from 0 to 255
- reference_mean: float32 [2], replicated, may hold values from -14 to -10
- loss_scale: float32 [], replicated, may hold values from 5120 to 20480
Outputs:
- hidden_grad: bfloat16 [256, 2, 5120], P('ctx', None, 'vocab')
- gain_grad: float32 [5120], P('vocab')
- head_grad: bfloat16 [5120, 81920], P('ctx', 'vocab')
- dpo_loss: float32 [], replicated
Inputs may be any that keep to these rules, and one draw needn't show every extreme that they name: `head`: every entry lies within 14 / sqrt(5120) of zero.
All inputs are finite; a program needn't handle non-finite values.
Results may differ from a plain program's by a relative error of at most 0.0057.
Values may be sent and summed in bfloat16 or wider, within the bound.
No kernel may reach another device: no remote copies, remote signals or barrier semaphores. Data moves between devices by JAX's collectives and lax.ppermute only.
A program may use at most 384 MiB of HBM per device.

v0:
```python
import jax
import jax.numpy as jnp
from jax import lax
from jax.sharding import PartitionSpec as P

EPSILON = 1e-06
BETA = 1.0


def on_device(hidden, gain, head, targets, prompt_length, reference_mean, loss_scale):
    tok_dev, seq_pair, model_width = hidden.shape
    slice_width, vocab_dev = head.shape
    vocab_count = lax.axis_size("vocab")
    rows_dev = tok_dev * seq_pair
    hidden_wide = hidden.astype(jnp.float32)
    inv_rms = lax.rsqrt(jnp.mean(hidden_wide * hidden_wide, axis=-1, keepdims=True) + EPSILON)
    unit_rows = hidden_wide * inv_rms
    gain_wide = gain.astype(jnp.float32)
    normed = (unit_rows * gain_wide).astype(jnp.bfloat16)
    spread = lax.all_to_all(normed, "ctx", split_axis=2, concat_axis=0, tiled=True)
    all_rows = spread.reshape(-1, slice_width)
    row_block = all_rows
    logits = lax.psum_scatter(
        jnp.dot(row_block, head, preferred_element_type=jnp.float32),
        "ctx",
        scatter_dimension=0,
        tiled=True,
    )
    vocab_start = lax.axis_index("vocab") * vocab_dev
    local_target = targets.reshape(-1) - vocab_start
    target_hit = lax.broadcasted_iota(jnp.int32, (rows_dev, vocab_dev), 1) == local_target[:, None]
    target_piece = jnp.sum(jnp.where(target_hit, logits, 0.0), axis=-1)
    row_top = lax.pmax(jnp.max(logits, axis=-1), "vocab")
    row_total, target_logit = lax.psum(
        (jnp.sum(jnp.exp(logits - row_top[:, None]), axis=-1), target_piece), "vocab"
    )
    log_norm = row_top + jnp.log(row_total)
    token_logp = (target_logit - log_norm).reshape(tok_dev, seq_pair)
    positions = lax.axis_index("ctx") * tok_dev + lax.broadcasted_iota(
        jnp.int32, (tok_dev, seq_pair), 0
    )
    loss_mask = (positions >= prompt_length[None, :]).astype(jnp.float32)
    seq_sums, seq_counts = lax.psum(
        (jnp.sum(loss_mask * token_logp, axis=0), jnp.sum(loss_mask, axis=0)), "ctx"
    )
    seq_means = seq_sums / seq_counts
    margin = BETA * (seq_means[0] - reference_mean[0] - (seq_means[1] - reference_mean[1]))
    dpo_loss = jax.nn.softplus(-margin)
    sig_pull = BETA * jax.nn.sigmoid(-margin)
    seq_weight = loss_scale * jnp.stack([-sig_pull, sig_pull]) / seq_counts
    row_weight = (seq_weight[None, :] * loss_mask).reshape(-1)
    row_probs = jnp.exp(logits - log_norm[:, None])
    logit_grad = (row_weight[:, None] * (target_hit.astype(jnp.float32) - row_probs)).astype(
        jnp.bfloat16
    )
    shard_rows = lax.all_gather(logit_grad, "ctx", axis=0, tiled=True)
    row_block = all_rows
    head_acc = lax.dot_general(
        row_block, shard_rows, (((0,), (0,)), ((), ())), preferred_element_type=jnp.float32
    )
    back_rows = lax.dot_general(
        shard_rows, head, (((1,), (1,)), ((), ())), preferred_element_type=jnp.float32
    )
    grad_rows = back_rows
    head_acc, grad_rows = (head_acc, grad_rows)
    head_grad = head_acc.astype(jnp.bfloat16)
    grad_cube = grad_rows.reshape(-1, seq_pair, slice_width)
    col_share = model_width // vocab_count
    col_start = lax.axis_index("vocab") * col_share
    summed = lax.psum(grad_cube, "vocab")
    normed_grad = lax.all_to_all(summed, "ctx", split_axis=0, concat_axis=2, tiled=True)
    upstream = normed_grad * gain_wide
    inner_mean = jnp.mean(upstream * unit_rows, axis=-1, keepdims=True)
    full_grad = inv_rms * (upstream - unit_rows * inner_mean)
    hidden_grad = lax.dynamic_slice_in_dim(full_grad, col_start, col_share, 2).astype(jnp.bfloat16)
    gain_part = lax.dynamic_slice_in_dim(
        jnp.sum(normed_grad * unit_rows, axis=(0, 1)), col_start, col_share, 0
    )
    gain_grad = lax.psum(gain_part, "ctx")
    return (hidden_grad, gain_grad, head_grad, dpo_loss)


def solution(mesh):
    in_specs = (P("ctx", None, None), P(), P("ctx", "vocab"), P("ctx", None), P(), P(), P())
    out_specs = (P("ctx", None, "vocab"), P("vocab"), P("ctx", "vocab"), P())
    return jax.shard_map(
        on_device, mesh=mesh, in_specs=in_specs, out_specs=out_specs, check_vma=False
    )
```

profile of v0, /device:TPU:1, one launch (start us, length us, event | category | flops | bytes accessed | tf_op | source)
XLA Modules:
  0.0 1338.5 jit_solution(3483741465404562202)
XLA Ops:
  7.2 7.7 copy.27
  15.0 6.6 fusion
  21.6 15.7 %convert_multiply_fusion = (f32[64,2,5120]{0,1,2:T(2,128)}, bf16[64,2,5120]{0,1,2:T(2,128)(2,1)}) fusion(bf16[64,2,5120]{0,1,2:T(2,128)(2,1)S(1)} %copy-done.1, f32[64,2]{0,1:T(2,128)S(1)} %add_rsqrt_fusion, f32[5120]{0:T(1024)S(1)} %convert_element_type.25), kind=kLoop, calls=%fused_computation.1 | loop fusion | flops 2621440 | bytes 5263872 | tf_op jit(solution)/shard_map/mul | solution.py:17
  37.3 4.7 reshape.81
  42.0 23.8 %all_to_all.33 = bf16[4,2,81920]{2,1,0:T(2,128)(2,1)} all-to-all(bf16[4,2,81920]{2,1,0:T(2,128)(2,1)} %reshape.81), channel_id=1, replica_groups=mesh['ctx'=4,'vocab'=64] {'ctx'}, dimensions={0} | all-to-all | bytes 2621440 | tf_op jit(solution)/shard_map/all_to_all | solution.py:20
  65.8 4.6 reshape.82
  70.4 7.5 copy.29
  77.9 4.1 reshape.73
  82.0 4.7 fusion.10
  86.7 0.6 copy-done.5
  87.4 0.1 sub.52
  88.2 35.5 %reduce-scatter.2.cloned.1.call-done = f32[128,1280]{1,0:T(8,128)} async-done(((f32[512,1280]{1,0:T(8,128)}), f32[128,1280]{1,0:T(8,128)}) %reduce-scatter.2.cloned.1.call-update) | async-done | bytes 655376 | tf_op jit(solution)/shard_map/reduce_scatter | solution.py:23
  123.7 1.2 reduce_max.9
  124.9 156.1 %pmax.7 = f32[128]{0:T(128)S(1)} all-reduce(f32[128]{0:T(128)S(1)} %reduce_max.9), channel_id=1, replica_groups=mesh['ctx'=4,'vocab'=64] {'vocab'}, use_global_device_ids=true, to_apply=%region_5.6 | all-reduce | flops 128 | bytes 1024 | tf_op jit(solution)/shard_map/pmax | solution.py:33
  281.1 1.4 select_reduce_fusion
  282.4 148.9 %all-reduce = (f32[128]{0:T(128)S(1)}, f32[128]{0:T(128)S(1)}) all-reduce(f32[128]{0:T(128)S(1)} %get-tuple-element.15, f32[128]{0:T(128)S(1)} %get-tuple-element.14), channel_id=1, replica_groups=mesh['ctx'=4,'vocab'=64] {'vocab'}, use_global_device_ids=true, to_apply=%region_7.8 | all-reduce | flops 256 | bytes 2048 | tf_op jit(solution)/shard_map/psum | solution.py:34
  431.6 60.8 %all-reduce.1 = (f32[2]{0:T(128)S(1)}, f32[2]{0:T(128)S(1)}) all-reduce(f32[2]{0:T(128)S(1)} %get-tuple-element.17, f32[2]{0:T(128)S(1)} %get-tuple-element.16), channel_id=1, replica_groups=mesh['ctx'=4,'vocab'=64] {'ctx'}, use_global_device_ids=true, to_apply=%region_11.12 | all-reduce | flops 4 | bytes 32 | tf_op jit(solution)/shard_map/psum | solution.py:43
  492.5 0.6 fusion.8
  495.9 0.1 mul.93
  496.0 2.1 multiply_convert_fusion.1
  498.2 22.2 %all-gather.2.cloned.1.call-done = bf16[512,1280]{1,0:T(8,128)(2,1)} async-done(((bf16[128,1280]{1,0:T(8,128)(2,1)}), bf16[512,1280]{1,0:T(8,128)(2,1)}) %all-gather.2.cloned.1.call-update) | async-done | bytes 1310736 | tf_op jit(solution)/shard_map/all_gather | solution.py:56
  520.4 4.7 fusion.11
  525.1 4.4 reshape.75
  529.5 660.1 %all-reduce.4.cloned.1.call-done = f32[256,2,1280]{2,1,0:T(2,128)} async-done(((f32[256,2,1280]{2,1,0:T(2,128)}), f32[256,2,1280]{2,1,0:T(2,128)}) %all-reduce.4.cloned.1.call-update) | async-done | bytes 2621456 | tf_op jit(solution)/shard_map/psum | solution.py:70
  1189.6 50.5 %all-to-all-start.1 = ((f32[256,2,1280]{2,1,0:T(2,128)}), f32[256,2,1280]{2,1,0:T(2,128)}, u32[]{:S(2)}, u32[]{:S(2)}) async-start(f32[256,2,1280]{2,1,0:T(2,128)} %all-reduce.4.cloned.1.call-done), calls=%async_computation.2 | async-start | bytes 5242880 | tf_op jit(solution)/shard_map/all_to_all | solution.py:71
  1240.2 5.3 convolution_convert_fusion
  1245.6 25.1 %all-to-all-done.1 = f32[256,2,1280]{2,1,0:T(2,128)} async-done(((f32[256,2,1280]{2,1,0:T(2,128)}), f32[256,2,1280]{2,1,0:T(2,128)}, u32[]{:S(2)}, u32[]{:S(2)}) %all-to-all-start.1) | async-done | bytes 2621472 | tf_op jit(solution)/shard_map/all_to_all | solution.py:71
  1270.7 8.1 copy.30
  1278.8 44.0 %fusion.1 = (f32[5120]{0:T(1024)S(1)}, f32[64,2]{0,1:T(2,128)S(1)}, f32[64,2,5120]{0,1,2:T(2,128)S(1)}) fusion(f32[4,64,2,1280]{1,2,3,0:T(2,128)} %copy.30, f32[64,2]{0,1:T(2,128)S(1)} %add_rsqrt_fusion, bf16[64,2,5120]{0,1,2:T(2,128)(2,1)} %copy.27, f32[5120]{0:T(1024)S(1)} %convert_element_type.25), kind=kLoop, calls=%fused_computation.6 | loop fusion | flops 4582272 | bytes 6595584 | tf_op jit(solution)/shard_map/reduce_sum | solution.py:77
  1322.7 0.9 fusion.3
  1323.7 0.7 copy.31
  1324.5 6.4 psum.47
  (30 shorter events, 0.8 us)
Async XLA Ops:
  7.2 74.8 %copy-start = (bf16[1280,1280]{1,0:T(8,128)(2,1)S(1)}, bf16[1280,1280]{1,0:T(8,128)(2,1)}, u32[]{:S(2)}) copy-start(bf16[1280,1280]{1,0:T(8,128)(2,1)} %param.9) | copy-start | bytes 9830404
  7.2 14.4 %copy-start.2 = (bf16[5120]{0:T(1024)(128)(2,1)S(1)}, bf16[5120]{0:T(1024)(128)(2,1)}, u32[]{:S(2)}) copy-start(bf16[5120]{0:T(1024)(128)(2,1)} %param.8) | copy-start | bytes 30724
  7.2 116.5 %reduce-scatter.2.cloned.1.call-start = ((), (), s32[]{:S(2)}) async-start(), calls=%async_computation.3 | async-start | bytes 3276800 | tf_op jit(solution)/shard_map/reduce_scatter | solution.py:23
  15.0 6.7 copy-start.1
  86.6 0.7 copy-start.5
  86.6 344.9 %copy-start.3 = (s32[2]{0:T(128)S(1)}, s32[2]{0:T(128)}, u32[]{:S(2)}) copy-start(s32[2]{0:T(128)} %param.11) | copy-start | bytes 28
  86.6 405.8 %copy-start.4 = (f32[2]{0:T(128)S(1)}, f32[2]{0:T(128)}, u32[]{:S(2)}) copy-start(f32[2]{0:T(128)} %param.12) | copy-start | bytes 28
  86.7 433.8 %all-gather.2.cloned.1.call-start = ((), (), s32[]{:S(2)}) async-start(), calls=%async_computation.4 | async-start | bytes 1638400 | tf_op jit(solution)/shard_map/all_gather | solution.py:56
  498.2 691.5 %all-reduce.4.cloned.1.call-start = ((), (), s32[]{:S(2)}) async-start(), calls=%async_computation.5 | async-start | bytes 5242880 | tf_op jit(solution)/shard_map/psum | solution.py:70
  1189.6 81.1 %all-to-all-start.1 = ((f32[256,2,1280]{2,1,0:T(2,128)}), f32[256,2,1280]{2,1,0:T(2,128)}, u32[]{:S(2)}, u32[]{:S(2)}) async-start(f32[256,2,1280]{2,1,0:T(2,128)} %all-reduce.4.cloned.1.call-done), calls=%async_computation.2 | async-start | bytes 5242880 | tf_op jit(solution)/shard_map/all_to_all | solution.py:71
Sparse Core Ops, SparseCore 0:
  86.8 36.8 reduce-scatter.1
  498.3 22.1 all-gather.1
  529.7 659.9 all-reduce.3
where the time goes:
time: 1340 us
  waiting for transfers between devices  743 us (55%)
  blocking collectives  396 us (30%)
  other arithmetic  72.2 us (5%)
  starting transfers between devices  50.6 us (4%)
  local copies, waits for them, and re-layouts  43.5 us (3%)
  between operations  18.4 us (1%)
  matrix products  14.7 us (1%)
    psum x1, waiting for transfers between devices, on_device(): summed = lax.psum(grad_cube, 'vocab')  660 us
    pmax x1, blocking collectives, on_device(): row_top = lax.pmax(jnp.max(logits, axis=-1), 'vocab')  156 us
    psum x1, blocking collectives, on_device(): lax.psum((jnp.sum(jnp.exp(logits - row_top[:, None]), axis=-1), target_pi...  149 us
    psum x1, blocking collectives, on_device(): lax.psum((jnp.sum(loss_mask * token_logp, axis=0), jnp.sum(loss_mask, axi...  60.8 us
    all_to_all x1, starting transfers between devices, on_device(): lax.all_to_all(summed, 'ctx', split_axis=0, concat_axis=2, tiled=True)  50.5 us
    reduce_sum x1, other arithmetic, on_device(): jnp.sum(normed_grad * unit_rows, axis=(0, 1))  44 us
    reduce_scatter x1, waiting for transfers between devices, on_device(): lax.psum_scatter(jnp.dot(row_block, head, preferred_element_type=jnp.floa...  35.5 us
  transfers between devices with their start and end apart: 4, of which 4 were waited for; matrix products, arithmetic and copies ran while one was open for 0% of the time, Pallas kernels for 0%

commit v1 on v0

v1 whole, which is shorter than its diff:
```python
from functools import partial

import jax
import jax.numpy as jnp
from jax import lax
from jax.experimental import pallas as pl
from jax.experimental.pallas import tpu as pltpu
from jax.sharding import Mesh, PartitionSpec as P

EPSILON = 1e-06
BETA = 1.0
SIZES = {"xl": 2, "co": 2, "z": 8, "y": 4, "xh": 2}
CTX = ("xl", "co")
VOC = ("z", "y", "xh")
F32 = jnp.float32
BF16 = jnp.bfloat16


def core_swap(x):
    return lax.ppermute(x, "co", [(0, 1), (1, 0)])


def chip_swap(x):
    return lax.ppermute(x, "xl", [(0, 1), (1, 0)])


def x_ring(x, cross):
    perm = []
    for xl in range(2):
        for co in range(2):
            for xh in range(2):
                to = (2 * xh + xl + (1 if co else -1)) % 4
                core = 1 - co if cross else co
                perm.append(((xl * 2 + co) * 2 + xh, ((to % 2) * 2 + core) * 2 + to // 2))
    return lax.ppermute(x, ("xl", "co", "xh"), perm)


def to_owner(x):
    perm = []
    for c in range(4):
        for z in range(8):
            for y in range(4):
                for xh in range(2):
                    source = ((c * 8 + z) * 4 + y) * 2 + xh
                    dest = (((y ^ c) * 8 + 2 * c + z // 4) * 4 + z % 4) * 2 + xh
                    perm.append((source, dest))
    return lax.ppermute(x, ("xl", "co", "z", "y", "xh"), perm)


def back_kernel(head_ref, g0, g1, g2, g3, out_ref):
    rows = g0.shape[0]
    for pair, (a, b) in enumerate(((g0, g1), (g2, g3))):
        both = jnp.concatenate([a[...], b[...]], axis=0)
        acc = lax.dot_general(
            head_ref[...], both, (((1,), (1,)), ((), ())), preferred_element_type=F32
        ).astype(BF16)
        out_ref[2 * pair] = acc[:, :rows]
        out_ref[2 * pair + 1] = acc[:, rows:]


def back_blocks(head, gs):
    feats, vocab = head.shape
    rows = gs[0].shape[0]
    block = 256
    whole = pl.BlockSpec((rows, vocab), lambda i: (0, 0))
    return pl.pallas_call(
        back_kernel,
        grid=(feats // block,),
        in_specs=[pl.BlockSpec((block, vocab), lambda i: (i, 0))] + [whole] * 4,
        out_specs=pl.BlockSpec((4, block, rows), lambda i: (0, i, 0)),
        out_shape=jax.ShapeDtypeStruct((4, feats, rows), BF16),
        compiler_params=pltpu.CompilerParams(vmem_limit_bytes=48 * 1024 * 1024),
    )(head, *gs)


def head_kernel(w_ref, n0, n1, n2, n3, g0, g1, g2, g3, out_ref):
    half = n0.shape[0] // 2
    total = None
    for s in range(2):
        rows = slice(s * half, (s + 1) * half)
        n_s = jnp.concatenate([n[rows, :] for n in (n0, n1, n2, n3)], axis=0)
        g_s = jnp.concatenate([g[rows, :] for g in (g0, g1, g2, g3)], axis=0)
        part = w_ref[s] * lax.dot_general(
            n_s, g_s, (((0,), (0,)), ((), ())), preferred_element_type=F32
        )
        total = part if total is None else total + part
    out_ref[...] = total.astype(BF16)


def head_blocks(weight, ns, gs):
    rows, feats = ns[0].shape
    vocab = gs[0].shape[1]
    block = 256
    return pl.pallas_call(
        head_kernel,
        grid=(feats // block,),
        in_specs=[pl.BlockSpec(memory_space=pltpu.SMEM)]
        + [pl.BlockSpec((rows, block), lambda i: (0, i))] * 4
        + [pl.BlockSpec((rows, vocab), lambda i: (0, 0))] * 4,
        out_specs=pl.BlockSpec((block, vocab), lambda i: (i, 0)),
        out_shape=jax.ShapeDtypeStruct((feats, vocab), BF16),
        compiler_params=pltpu.CompilerParams(vmem_limit_bytes=48 * 1024 * 1024),
    )(weight, *ns, *gs)


def on_device(hidden, gain, head, targets, prompt_length, reference_mean, loss_scale):
    tok_dev, seq_pair, model_width = hidden.shape
    feats, vocab_dev = head.shape
    rows = tok_dev * seq_pair
    ctx = lax.axis_index(CTX)
    voc = lax.axis_index(VOC)

    wide = hidden.astype(F32)
    inv_rms = lax.rsqrt(jnp.mean(wide * wide, axis=-1, keepdims=True) + EPSILON)
    gain_wide = gain.astype(F32)
    normed = (wide * inv_rms * gain_wide).astype(BF16)
    normed = normed.transpose(1, 0, 2).reshape(rows, model_width)

    def part(k):
        return lax.dynamic_slice_in_dim(normed, (ctx ^ k) * feats, feats, 1)

    n_own = part(0)
    n_sib = core_swap(part(1))
    n_far = x_ring(part(2), False)
    n_far_sib = x_ring(part(3), True)

    def logits_of(n):
        return jnp.dot(n, head, preferred_element_type=F32)

    far = logits_of(n_far) + core_swap(logits_of(n_far_sib))
    near = logits_of(n_own) + core_swap(logits_of(n_sib))
    logits = near + chip_swap(far)

    flat_targets = targets.T.reshape(rows)
    local_target = flat_targets - voc * vocab_dev
    hit = lax.broadcasted_iota(jnp.int32, (rows, vocab_dev), 1) == local_target[:, None]
    top = jnp.max(logits, axis=-1)
    below = logits - top[:, None]
    exps = jnp.exp(below)
    stats = jnp.stack(
        [
            top,
            jnp.sum(exps, axis=-1),
            jnp.sum(exps * below, axis=-1),
            jnp.sum(jnp.where(hit, logits, 0.0), axis=-1),
        ]
    )
    shards = lax.all_to_all(
        jnp.broadcast_to(stats[None], (64,) + stats.shape), VOC, 0, 0
    )
    tops, sums, dots, picks = shards[:, 0], shards[:, 1], shards[:, 2], shards[:, 3]
    row_top = jnp.max(tops, axis=0)
    shift = tops - row_top
    scale = jnp.exp(shift)
    row_total = jnp.sum(scale * sums, axis=0)
    row_dot = jnp.sum(scale * (dots + sums * shift), axis=0)
    target_logit = jnp.sum(picks, axis=0)
    log_norm = row_top + jnp.log(row_total)

    positions = ctx * tok_dev + lax.broadcasted_iota(jnp.int32, (seq_pair, tok_dev), 1)
    mask = (positions >= prompt_length[:, None]).astype(F32)
    row_mask = mask.reshape(rows)
    grad = (row_mask[:, None] * (hit.astype(F32) - jnp.exp(logits - log_norm[:, None]))).astype(
        BF16
    )
    g_far = chip_swap(grad)
    g_sib = core_swap(grad)
    g_far_sib = core_swap(g_far)
    gs = (grad, g_sib, g_far, g_far_sib)

    token_logp = (target_logit - log_norm).reshape(seq_pair, tok_dev)
    seq_sums = jnp.sum(mask * token_logp, axis=1)
    seq_sums = seq_sums + core_swap(seq_sums)
    seq_sums = seq_sums + chip_swap(seq_sums)
    every = lax.broadcasted_iota(jnp.int32, (seq_pair, 4 * tok_dev), 1)
    seq_counts = jnp.sum((every >= prompt_length[:, None]).astype(F32), axis=1)
    seq_means = seq_sums / seq_counts
    margin = BETA * (seq_means[0] - reference_mean[0] - (seq_means[1] - reference_mean[1]))
    dpo_loss = jax.nn.softplus(-margin)
    sig_pull = BETA * jax.nn.sigmoid(-margin)
    seq_weight = loss_scale * jnp.stack([-sig_pull, sig_pull]) / seq_counts

    back = back_blocks(head, gs)
    head_grad = head_blocks(seq_weight, (n_own, n_sib, n_far, n_far_sib), gs)
    over_y = lax.all_to_all(back, "y", 0, 0)
    part_y = jnp.sum(over_y.astype(F32), axis=0).astype(BF16)
    over_zx = lax.all_to_all(part_y.reshape(16, feats // 16, rows), ("z", "xh"), 0, 0)
    normed_grad = to_owner(jnp.sum(over_zx.astype(F32), axis=0))

    share = feats // 16
    row_weight = jnp.broadcast_to(seq_weight[:, None], (seq_pair, tok_dev)).reshape(rows)
    normed_grad = normed_grad * row_weight
    inner_mean = (
        row_weight * row_mask * (target_logit - row_top - row_dot / row_total) / model_width
    )
    inv_row = inv_rms[:, :, 0].T.reshape(rows)
    gain_own = lax.dynamic_slice_in_dim(gain_wide, voc * share, share, 0)
    mine = lax.dynamic_slice_in_dim(hidden, voc * share, share, 2)
    unit = mine.transpose(2, 1, 0).reshape(share, rows).astype(F32) * inv_row
    hidden_grad = (inv_row * (normed_grad * gain_own[:, None] - unit * inner_mean)).astype(BF16)
    hidden_grad = hidden_grad.reshape(share, seq_pair, tok_dev).transpose(2, 1, 0)
    gain_grad = jnp.sum(normed_grad * unit, axis=1)
    gain_grad = gain_grad + core_swap(gain_grad)
    gain_grad = gain_grad + chip_swap(gain_grad)
    return (hidden_grad, gain_grad, head_grad, dpo_loss)


def solution(mesh):
    fine = Mesh(mesh.devices.reshape(tuple(SIZES.values())), tuple(SIZES))
    in_specs = (P(CTX, None, None), P(), P(CTX, VOC), P(CTX, None), P(), P(), P())
    out_specs = (P(CTX, None, VOC), P(VOC), P(CTX, VOC), P())
    return jax.shard_map(
        on_device, mesh=fine, in_specs=in_specs, out_specs=out_specs, check_vma=False
    )
```

time: 1340 us -> 158 us (0.12)
  waiting for transfers between devices: 743 us -> 65.8 us
  blocking collectives: 396 us -> 0 us
  other arithmetic: 72.2 us -> 14.9 us
  local copies, waits for them, and re-layouts: 43.5 us -> 13.9 us
    psum x1 -> x0, waiting for transfers between devices: 660 us -> none  [on_device(): summed = lax.psum(grad_cube, 'vocab')]
    psum x3 -> x0, blocking collectives: 216 us -> none  [the longest x1 149 us: on_device(): lax.psum((jnp.sum(jnp.exp(logits - row_top[:, None]), axis=-1), target_pi...]
    pmax x1 -> x0, blocking collectives: 156 us -> none  [on_device(): row_top = lax.pmax(jnp.max(logits, axis=-1), 'vocab')]
    reduce_sum x4 -> x9, other arithmetic: 52.1 us -> 6.75 us  [the longest x1 2.75 us: on_device(): inv_rms = lax.rsqrt(jnp.mean(wide * wide, axis=-1, keepdims=True) + EPSILON)]
    ppermute x0 -> x14, waiting for transfers between devices: none -> 35.7 us  [the longest x4 19.8 us: chip_swap(): return lax.ppermute(x, 'xl', [(0, 1), (1, 0)])]
    reduce_scatter x1 -> x0, waiting for transfers between devices: 35.5 us -> none  [on_device(): lax.psum_scatter(jnp.dot(row_block, head, preferred_element_type=jnp.floa...]
    all_to_all x1 -> x3, starting transfers between devices: 50.5 us -> 18 us  [the longest x1 10.1 us: on_device(): lax.all_to_all(jnp.broadcast_to(stats[None], (64,) + stats.shape), VOC, 0...]
    ppermute x0 -> x14, starting transfers between devices: none -> 25.6 us  [the longest x7 14.1 us: core_swap(): return lax.ppermute(x, 'co', [(0, 1), (1, 0)])]
  transfers between devices with their start and end apart: 4 -> 17, of which waited for: 4 -> 12; matrix products, arithmetic and copies ran while one was open for 0% -> 6% of each run, Pallas kernels for 0% -> 3%
where the time goes in v1:
time: 158 us; the launch traced here: 156 us
  waiting for transfers between devices  65.8 us (42%)
  starting transfers between devices  43.6 us (28%)
  other arithmetic  14.9 us (9%)
  local copies, waits for them, and re-layouts  13.9 us (9%)
  Pallas kernels  7.5 us (5%)
  between operations  5.49 us (3%)
  matrix products  5.13 us (3%)
    ppermute x4, waiting for transfers between devices, chip_swap(): return lax.ppermute(x, 'xl', [(0, 1), (1, 0)])  19.8 us
    all_to_all x1, waiting for transfers between devices, on_device(): over_y = lax.all_to_all(back, 'y', 0, 0)  16.4 us
    ppermute x7, starting transfers between devices, core_swap(): return lax.ppermute(x, 'co', [(0, 1), (1, 0)])  14.1 us
    all_to_all x1, waiting for transfers between devices, on_device(): lax.all_to_all(jnp.broadcast_to(stats[None], (64,) + stats.shape), VOC, 0...  11.3 us
    all_to_all x1, starting transfers between devices, on_device(): lax.all_to_all(jnp.broadcast_to(stats[None], (64,) + stats.shape), VOC, 0...  10.1 us
    ppermute x2, waiting for transfers between devices, x_ring(): return lax.ppermute(x, ('xl', 'co', 'xh'), perm)  8.75 us
    unnamed x43, local copies, waits for them, and re-layouts  6.28 us
    ppermute x4, starting transfers between devices, chip_swap(): return lax.ppermute(x, 'xl', [(0, 1), (1, 0)])  5.9 us
  transfers between devices with their start and end apart: 17, of which 12 were waited for; matrix products, arithmetic and copies ran while one was open for 6% of the time, Pallas kernels for 3%

profile of v1, /device:TPU:1, one launch (start us, length us, event | category | flops | bytes accessed | tf_op | source)
XLA Modules:
  0.0 156.3 jit_solution(9801358531786142513)
XLA Ops:
  1.4 2.8 %fusion = f32[64,2]{1,0:T(8,128)S(1)} fusion(bf16[64,2,5120]{2,1,0:T(2,128)(2,1)} %param.7), kind=kLoop, calls=%fused_computation.2 | loop fusion | flops 1965952 | bytes 1311232 | tf_op jit(solution)/shard_map/reduce_sum | solution.py:114
  4.1 2.8 %fusion.3 = bf16[2,64,5120]{2,0,1:T(2,128)(2,1)S(1)} fusion(bf16[64,2,5120]{2,1,0:T(2,128)(2,1)} %param.7, f32[5120]{0:T(1024)S(1)} %convert_element_type.47, f32[64,2]{1,0:T(8,128)S(1)} %get-tuple-element.42), kind=kLoop, calls=%fused_computation.6 | loop fusion | flops 2621440 | bytes 2642432 | tf_op jit(solution)/shard_map/transpose | solution.py:117
  7.0 1.3 copy.34
  8.3 2.2 %constant_dynamic-slice_fusion.2 = (bf16[128,1280]{1,0:T(8,128)(2,1)S(1)}, bf16[128,1280]{1,0:T(8,128)(2,1)S(1)}, bf16[128,1280]{1,0:T(8,128)(2,1)S(1)}, bf16[128,1280]{1,0:T(8,128)(2,1)}) fusion(bf16[128,5120]{1,0:T(8,128)(2,1)} %bitcast.35, s32[]{:T(128)S(6)} %select_n.25, s32[]{:T(128)S(6)} %select_n.27, s32[]{:T(128)S(6)} %select_n.26, s32[]{:T(128)S(6)} %select_n.24), kind=kLoop, calls=%fused_computation.26 | loop fusion | bytes 2621456 | tf_op jit(solution)/shard_map/dynamic_slice | solution.py:120
  10.5 2.6 %collective-permute-start.3 = (bf16[128,1280]{1,0:T(8,128)(2,1)S(1)}, bf16[128,1280]{1,0:T(8,128)(2,1)S(1)}, u32[]{:S(2)}, u32[]{:S(2)}) collective-permute-start(bf16[128,1280]{1,0:T(8,128)(2,1)S(1)} %get-tuple-element.32), channel_id=1, source_target_pairs={{0,193},{1,192},{64,128},{65,129},{128,64},{129,65},{192,1},{193,0... | collective-permute-start | bytes 983048 | tf_op jit(solution)/shard_map/ppermute | solution.py:35
  14.2 3.9 %collective-permute-done.3.n3 = bf16[128,1280]{1,0:T(8,128)(2,1)S(1)} collective-permute-done((bf16[128,1280]{1,0:T(8,128)(2,1)S(1)}, bf16[128,1280]{1,0:T(8,128)(2,1)S(1)}, u32[]{:S(2)}, u32[]{:S(2)}) %collective-permute-start.3) | collective-permute-done | bytes 327712 | tf_op jit(solution)/shard_map/ppermute | solution.py:35
  18.8 3.4 %collective-permute-start.4 = (f32[128,1280]{1,0:T(8,128)S(1)}, f32[128,1280]{1,0:T(8,128)S(1)}, u32[]{:S(2)}, u32[]{:S(2)}) collective-permute-start(f32[128,1280]{1,0:T(8,128)S(1)} %fusion.15), channel_id=1, source_target_pairs={{0,64},{64,0},{1,65},{65,1},{2,66},{66,2},{3,67},{67,3},{4,68},{68... | collective-permute-start | bytes 1966088 | tf_op jit(solution)/shard_map/ppermute | solution.py:20
  22.2 1.5 fusion.14
  24.5 4.8 %collective-permute-done.2.n2 = bf16[128,1280]{1,0:T(8,128)(2,1)S(1)} collective-permute-done((bf16[128,1280]{1,0:T(8,128)(2,1)S(1)}, bf16[128,1280]{1,0:T(8,128)(2,1)S(1)}, u32[]{:S(2)}, u32[]{:S(2)}) %collective-permute-start.2) | collective-permute-done | bytes 327712 | tf_op jit(solution)/shard_map/ppermute | solution.py:35
  29.3 1.5 convolution_add_fusion
  31.6 1.6 %fusion.13 = f32[128,1280]{1,0:T(8,128)S(1)} fusion(bf16[128,1280]{1,0:T(8,128)(2,1)} %get-tuple-element.34.n0, bf16[1280,1280]{1,0:T(8,128)(2,1)S(1)} %copy-done), kind=kOutput, calls=%fused_computation.43 | convolution fusion | flops 419430400 | bytes 4259840 | tf_op jit(solution)/shard_map/dot_general | solution.py:128
  33.2 14.9 %collective-permute-done.5 = f32[128,1280]{1,0:T(8,128)} collective-permute-done((f32[128,1280]{1,0:T(8,128)}, f32[128,1280]{1,0:T(8,128)}, u32[]{:S(2)}, u32[]{:S(2)}) %collective-permute-start.5) | collective-permute-done | bytes 655392 | tf_op jit(solution)/shard_map/ppermute | solution.py:24
  48.2 1.5 fusion.9
  51.5 10.1 %all-to-all-start = ((f32[64,4,128]{2,1,0:T(4,128)}), f32[64,4,128]{2,1,0:T(4,128)S(1)}, u32[]{:S(2)}, u32[]{:S(2)}) async-start(f32[64,4,128]{2,1,0:T(4,128)} %broadcast_in_dim.9), calls=%async_computation | async-start | bytes 262144 | tf_op jit(solution)/shard_map/all_to_all | solution.py:148
  61.6 11.3 %all-to-all-done = f32[64,4,128]{2,1,0:T(4,128)S(1)} async-done(((f32[64,4,128]{2,1,0:T(4,128)}), f32[64,4,128]{2,1,0:T(4,128)S(1)}, u32[]{:S(2)}, u32[]{:S(2)}) %all-to-all-start) | async-done | bytes 131104 | tf_op jit(solution)/shard_map/all_to_all | solution.py:148
  74.8 1.4 multiply_convert_fusion.g0
  76.4 3.8 %collective-permute-start.6 = (bf16[128,1280]{1,0:T(8,128)(2,1)S(1)}, bf16[128,1280]{1,0:T(8,128)(2,1)S(1)}, u32[]{:S(2)}, u32[]{:S(2)}) collective-permute-start(bf16[128,1280]{1,0:T(8,128)(2,1)S(1)} %multiply_convert_fusion.g0), channel_id=1, source_target_pairs={{0,64},{64,0},{1,65},{65,1},{2,66},{66,2},{3,67},{67,3},{4,68},{68... | collective-permute-start | bytes 983048 | tf_op jit(solution)/shard_map/ppermute | solution.py:20
  80.2 2.6 %collective-permute-done.7.g2 = bf16[128,1280]{1,0:T(8,128)(2,1)S(1)} collective-permute-done((bf16[128,1280]{1,0:T(8,128)(2,1)S(1)}, bf16[128,1280]{1,0:T(8,128)(2,1)S(1)}, u32[]{:S(2)}, u32[]{:S(2)}) %collective-permute-start.7) | collective-permute-done | bytes 327712 | tf_op jit(solution)/shard_map/ppermute | solution.py:24
  82.8 3.6 %collective-permute-start.8 = (bf16[128,1280]{1,0:T(8,128)(2,1)S(1)}, bf16[128,1280]{1,0:T(8,128)(2,1)S(1)}, u32[]{:S(2)}, u32[]{:S(2)}) collective-permute-start(bf16[128,1280]{1,0:T(8,128)(2,1)S(1)} %collective-permute-done.7.g2), channel_id=1, source_target_pairs={{0,64},{64,0},{1,65},{65,1},{2,66},{66,2},{3,67},{67,3},{4,68},{68... | collective-permute-start | bytes 983048 | tf_op jit(solution)/shard_map/ppermute | solution.py:20
  86.4 1.3 collective-permute-done.8.g3
  87.7 2.8 %shard_map.102 = bf16[4,1280,128]{2,1,0:T(8,128)(2,1)S(1)} custom-call(bf16[1280,1280]{1,0:T(8,128)(2,1)S(1)} %copy-done, bf16[128,1280]{1,0:T(8,128)(2,1)S(1)} %multiply_convert_fusion.g0, bf16[128,1280]{1,0:T(8,128)(2,1)S(1)} %collective-permute-done.6.g1, bf16[128,1280]{1,0:T(8,128)(2,1)S(1)} %collective-permute-done.7.g2, ...), custom_call_target="tpu_custom_call" | custom-call | tf_op jit(solution)/shard_map/pallas_call | solution.py:66
  94.5 4.4 %all-to-all-start.1 = ((bf16[4,1280,128]{2,1,0:T(8,128)(2,1)}), bf16[4,1280,128]{2,1,0:T(8,128)(2,1)}, u32[]{:S(2)}, u32[]{:S(2)}) async-start(bf16[4,1280,128]{2,1,0:T(8,128)(2,1)} %copy-done.1), calls=%async_computation.1 | async-start | bytes 2621440 | tf_op jit(solution)/shard_map/all_to_all | solution.py:185
  100.2 16.4 %all-to-all-done.1 = bf16[4,1280,128]{2,1,0:T(8,128)(2,1)} async-done(((bf16[4,1280,128]{2,1,0:T(8,128)(2,1)}), bf16[4,1280,128]{2,1,0:T(8,128)(2,1)}, u32[]{:S(2)}, u32[]{:S(2)}) %all-to-all-start.1) | async-done | bytes 1310752 | tf_op jit(solution)/shard_map/all_to_all | solution.py:185
  116.7 2.3 %reduce_sum.116 = bf16[1280,128]{1,0:T(8,128)(2,1)} reduce(bf16[4,1280,128]{2,1,0:T(8,128)(2,1)} %all-to-all-done.1, bf16[]{:T(256)} %constant.54.clone.1), dimensions={0}, to_apply=%region_7.8 | reduce | flops 491520 | bytes 1638402 | tf_op jit(solution)/shard_map/reduce_sum | solution.py:186
  119.0 3.5 %all-to-all-start.2 = ((bf16[16,80,128]{2,1,0:T(8,128)(2,1)}), bf16[16,80,128]{2,1,0:T(8,128)(2,1)S(1)}, u32[]{:S(2)}, u32[]{:S(2)}) async-start(bf16[16,80,128]{2,1,0:T(8,128)(2,1)} %bitcast.10), calls=%async_computation.2 | async-start | bytes 655360 | tf_op jit(solution)/shard_map/all_to_all | solution.py:187
  124.8 1.3 collective-permute-start.10
  127.4 2.2 %collective-permute-done.11 = f32[2]{0:T(128)S(1)} collective-permute-done((f32[2]{0:T(128)S(1)}, f32[2]{0:T(128)S(1)}, u32[]{:S(2)}, u32[]{:S(2)}) %collective-permute-start.11) | collective-permute-done | bytes 40 | tf_op jit(solution)/shard_map/ppermute | solution.py:24
  133.1 2.3 %all-to-all-done.2 = bf16[16,80,128]{2,1,0:T(8,128)(2,1)S(1)} async-done(((bf16[16,80,128]{2,1,0:T(8,128)(2,1)}), bf16[16,80,128]{2,1,0:T(8,128)(2,1)S(1)}, u32[]{:S(2)}, u32[]{:S(2)}) %all-to-all-start.2) | async-done | bytes 327712 | tf_op jit(solution)/shard_map/all_to_all | solution.py:187
  135.4 3.0 %collective-permute-start.9 = (f32[80,128]{1,0:T(8,128)S(1)}, f32[80,128]{1,0:T(8,128)S(1)}, u32[]{:S(2)}, u32[]{:S(2)}) collective-permute-start(f32[80,128]{1,0:T(8,128)S(1)} %convert_reduce_fusion), channel_id=1, source_target_pairs={{0,0},{1,1},{2,64},{3,65},{4,128},{5,129},{6,192},{7,193},{8,2},{9... | collective-permute-start | bytes 122888 | tf_op jit(solution)/shard_map/ppermute | solution.py:47
  138.4 4.1 %collective-permute-done.9 = f32[80,128]{1,0:T(8,128)S(1)} collective-permute-done((f32[80,128]{1,0:T(8,128)S(1)}, f32[80,128]{1,0:T(8,128)S(1)}, u32[]{:S(2)}, u32[]{:S(2)}) %collective-permute-start.9) | collective-permute-done | bytes 40992 | tf_op jit(solution)/shard_map/ppermute | solution.py:47
  143.8 5.2 %collective-permute-start.13 = (f32[80]{0:T(128)S(1)}, f32[80]{0:T(128)S(1)}, u32[]{:S(2)}, u32[]{:S(2)}) collective-permute-start(f32[80]{0:T(128)S(1)} %add.110), channel_id=1, source_target_pairs={{0,128},{128,0},{1,129},{129,1},{2,130},{130,2},{3,131},{131,3},{4... | collective-permute-start | bytes 968 | tf_op jit(solution)/shard_map/ppermute | solution.py:24
  149.1 4.7 %shard_map.103 = bf16[1280,1280]{1,0:T(8,128)(2,1)} custom-call(f32[2]{0:T(128)S(1)} %fusion.6.w_ref, bf16[128,1280]{1,0:T(8,128)(2,1)S(1)} %copy-done.2, bf16[128,1280]{1,0:T(8,128)(2,1)S(1)} %copy-done.8, bf16[128,1280]{1,0:T(8,128)(2,1)S(1)} %copy-done.10, bf16[128,1280]{1,0:T(8,128)(2,1)S(1)} %copy-done.6, bf16[128,1280]{1,0:T(8,128)(2,1)S(1)} %copy-done.4, ...), custom_call_target="tpu_custom_call" | custom-call | tf_op jit(solution)/shard_map/pallas_call | solution.py:94
  (95 shorter events, 19.7 us)
Async XLA Ops:
  7.0 11.2 %copy-start = (bf16[1280,1280]{1,0:T(8,128)(2,1)S(1)}, bf16[1280,1280]{1,0:T(8,128)(2,1)}, u32[]{:S(2)}) copy-start(bf16[1280,1280]{1,0:T(8,128)(2,1)} %head_ref.1) | copy-start | bytes 9830404
  10.5 7.7 %collective-permute-start.3 = (bf16[128,1280]{1,0:T(8,128)(2,1)S(1)}, bf16[128,1280]{1,0:T(8,128)(2,1)S(1)}, u32[]{:S(2)}, u32[]{:S(2)}) collective-permute-start(bf16[128,1280]{1,0:T(8,128)(2,1)S(1)} %get-tuple-element.32), channel_id=1, source_target_pairs={{0,193},{1,192},{64,128},{65,129},{128,64},{129,65},{192,1},{193,0... | collective-permute-start | bytes 983048 | tf_op jit(solution)/shard_map/ppermute | solution.py:35
  13.1 9.1 %collective-permute-start = (bf16[128,1280]{1,0:T(8,128)(2,1)S(1)}, bf16[128,1280]{1,0:T(8,128)(2,1)S(1)}, u32[]{:S(2)}, u32[]{:S(2)}) collective-permute-start(bf16[128,1280]{1,0:T(8,128)(2,1)S(1)} %get-tuple-element.31), channel_id=1, source_target_pairs={{0,64},{64,0},{1,65},{65,1},{2,66},{66,2},{3,67},{67,3},{4,68},{68... | collective-permute-start | bytes 983048 | tf_op jit(solution)/shard_map/ppermute | solution.py:20
  18.2 5.5 %copy-start.5 = (bf16[128,1280]{1,0:T(8,128)(2,1)}, bf16[128,1280]{1,0:T(8,128)(2,1)S(1)}, u32[]{:S(2)}) copy-start(bf16[128,1280]{1,0:T(8,128)(2,1)S(1)} %collective-permute-done.3.n3) | copy-start | bytes 983044
  18.8 10.5 %collective-permute-start.4 = (f32[128,1280]{1,0:T(8,128)S(1)}, f32[128,1280]{1,0:T(8,128)S(1)}, u32[]{:S(2)}, u32[]{:S(2)}) collective-permute-start(f32[128,1280]{1,0:T(8,128)S(1)} %fusion.15), channel_id=1, source_target_pairs={{0,64},{64,0},{1,65},{65,1},{2,66},{66,2},{3,67},{67,3},{4,68},{68... | collective-permute-start | bytes 1966088 | tf_op jit(solution)/shard_map/ppermute | solution.py:20
  22.2 7.1 %collective-permute-start.2 = (bf16[128,1280]{1,0:T(8,128)(2,1)S(1)}, bf16[128,1280]{1,0:T(8,128)(2,1)S(1)}, u32[]{:S(2)}, u32[]{:S(2)}) collective-permute-start(bf16[128,1280]{1,0:T(8,128)(2,1)S(1)} %get-tuple-element.33), channel_id=1, source_target_pairs={{0,129},{1,128},{64,192},{65,193},{128,0},{129,1},{192,65},{193,64... | collective-permute-start | bytes 983048 | tf_op jit(solution)/shard_map/ppermute | solution.py:35
  22.2 8.6 %copy-start.7 = (bf16[128,1280]{1,0:T(8,128)(2,1)}, bf16[128,1280]{1,0:T(8,128)(2,1)S(1)}, u32[]{:S(2)}) copy-start(bf16[128,1280]{1,0:T(8,128)(2,1)S(1)} %collective-permute-done.n1) | copy-start | bytes 983044
  23.7 7.9 %copy-start.19 = (s32[64,2]{0,1:T(2,128)S(1)}, s32[64,2]{0,1:T(2,128)}, u32[]{:S(2)}) copy-start(s32[64,2]{0,1:T(2,128)} %param.10) | copy-start | bytes 1540
  23.7 9.6 %collective-permute-start.1 = (f32[128,1280]{1,0:T(8,128)}, f32[128,1280]{1,0:T(8,128)}, u32[]{:S(2)}, u32[]{:S(2)}) collective-permute-start(f32[128,1280]{1,0:T(8,128)} %fusion.14), channel_id=1, source_target_pairs={{0,64},{64,0},{1,65},{65,1},{2,66},{66,2},{3,67},{67,3},{4,68},{68... | collective-permute-start | bytes 1966088 | tf_op jit(solution)/shard_map/ppermute | solution.py:20
  31.5 16.7 %collective-permute-start.5 = (f32[128,1280]{1,0:T(8,128)}, f32[128,1280]{1,0:T(8,128)}, u32[]{:S(2)}, u32[]{:S(2)}) collective-permute-start(f32[128,1280]{1,0:T(8,128)} %convolution_add_fusion), channel_id=1, source_target_pairs={{0,128},{128,0},{1,129},{129,1},{2,130},{130,2},{3,131},{131,3},{4... | collective-permute-start | bytes 1966088 | tf_op jit(solution)/shard_map/ppermute | solution.py:24
  33.2 41.3 %copy-start.20 = (s32[2]{0:T(128)S(1)}, s32[2]{0:T(128)}, u32[]{:S(2)}) copy-start(s32[2]{0:T(128)} %param.11) | copy-start | bytes 28
  51.5 21.4 %all-to-all-start = ((f32[64,4,128]{2,1,0:T(4,128)}), f32[64,4,128]{2,1,0:T(4,128)S(1)}, u32[]{:S(2)}, u32[]{:S(2)}) async-start(f32[64,4,128]{2,1,0:T(4,128)} %broadcast_in_dim.9), calls=%async_computation | async-start | bytes 262144 | tf_op jit(solution)/shard_map/all_to_all | solution.py:148
  76.2 6.6 %collective-permute-start.7 = (bf16[128,1280]{1,0:T(8,128)(2,1)S(1)}, bf16[128,1280]{1,0:T(8,128)(2,1)S(1)}, u32[]{:S(2)}, u32[]{:S(2)}) collective-permute-start(bf16[128,1280]{1,0:T(8,128)(2,1)S(1)} %multiply_convert_fusion.g0), channel_id=1, source_target_pairs={{0,128},{128,0},{1,129},{129,1},{2,130},{130,2},{3,131},{131,3},{4... | collective-permute-start | bytes 983048 | tf_op jit(solution)/shard_map/ppermute | solution.py:24
  76.4 10.0 %collective-permute-start.6 = (bf16[128,1280]{1,0:T(8,128)(2,1)S(1)}, bf16[128,1280]{1,0:T(8,128)(2,1)S(1)}, u32[]{:S(2)}, u32[]{:S(2)}) collective-permute-start(bf16[128,1280]{1,0:T(8,128)(2,1)S(1)} %multiply_convert_fusion.g0), channel_id=1, source_target_pairs={{0,64},{64,0},{1,65},{65,1},{2,66},{66,2},{3,67},{67,3},{4,68},{68... | collective-permute-start | bytes 983048 | tf_op jit(solution)/shard_map/ppermute | solution.py:20
  82.8 4.9 %collective-permute-start.8 = (bf16[128,1280]{1,0:T(8,128)(2,1)S(1)}, bf16[128,1280]{1,0:T(8,128)(2,1)S(1)}, u32[]{:S(2)}, u32[]{:S(2)}) collective-permute-start(bf16[128,1280]{1,0:T(8,128)(2,1)S(1)} %collective-permute-done.7.g2), channel_id=1, source_target_pairs={{0,64},{64,0},{1,65},{65,1},{2,66},{66,2},{3,67},{67,3},{4,68},{68... | collective-permute-start | bytes 983048 | tf_op jit(solution)/shard_map/ppermute | solution.py:20
  90.5 1.1 copy-start.1
  94.5 28.1 %copy-start.18 = (f32[2]{0:T(128)S(1)}, f32[2]{0:T(128)}, u32[]{:S(2)}) copy-start(f32[2]{0:T(128)} %param.12) | copy-start | bytes 28
  94.5 54.6 %copy-start.2 = (bf16[128,1280]{1,0:T(8,128)(2,1)S(1)}, bf16[128,1280]{1,0:T(8,128)(2,1)}, u32[]{:S(2)}) copy-start(bf16[128,1280]{1,0:T(8,128)(2,1)} %get-tuple-element.34.n0) | copy-start | bytes 983044
  94.5 54.6 %copy-start.6 = (bf16[128,1280]{1,0:T(8,128)(2,1)S(1)}, bf16[128,1280]{1,0:T(8,128)(2,1)}, u32[]{:S(2)}) copy-start(bf16[128,1280]{1,0:T(8,128)(2,1)} %copy-done.5) | copy-start | bytes 983044
  94.5 54.6 %copy-start.8 = (bf16[128,1280]{1,0:T(8,128)(2,1)S(1)}, bf16[128,1280]{1,0:T(8,128)(2,1)}, u32[]{:S(2)}) copy-start(bf16[128,1280]{1,0:T(8,128)(2,1)} %copy-done.7) | copy-start | bytes 983044
  94.5 54.6 %copy-start.10 = (bf16[128,1280]{1,0:T(8,128)(2,1)S(1)}, bf16[128,1280]{1,0:T(8,128)(2,1)}, u32[]{:S(2)}) copy-start(bf16[128,1280]{1,0:T(8,128)(2,1)} %copy-done.9) | copy-start | bytes 983044
  94.5 22.2 %all-to-all-start.1 = ((bf16[4,1280,128]{2,1,0:T(8,128)(2,1)}), bf16[4,1280,128]{2,1,0:T(8,128)(2,1)}, u32[]{:S(2)}, u32[]{:S(2)}) async-start(bf16[4,1280,128]{2,1,0:T(8,128)(2,1)} %copy-done.1), calls=%async_computation.1 | async-start | bytes 2621440 | tf_op jit(solution)/shard_map/all_to_all | solution.py:185
  98.9 50.1 %copy-start.4 = (bf16[128,1280]{1,0:T(8,128)(2,1)S(1)}, bf16[128,1280]{1,0:T(8,128)(2,1)}, u32[]{:S(2)}) copy-start(bf16[128,1280]{1,0:T(8,128)(2,1)} %copy-done.3) | copy-start | bytes 983044
  99.0 50.1 %copy-start.12 = (bf16[128,1280]{1,0:T(8,128)(2,1)S(1)}, bf16[128,1280]{1,0:T(8,128)(2,1)}, u32[]{:S(2)}) copy-start(bf16[128,1280]{1,0:T(8,128)(2,1)} %copy-done.11) | copy-start | bytes 983044
  99.0 50.1 %copy-start.14 = (bf16[128,1280]{1,0:T(8,128)(2,1)S(1)}, bf16[128,1280]{1,0:T(8,128)(2,1)}, u32[]{:S(2)}) copy-start(bf16[128,1280]{1,0:T(8,128)(2,1)} %copy-done.13) | copy-start | bytes 983044
  99.0 50.1 %copy-start.16 = (bf16[128,1280]{1,0:T(8,128)(2,1)S(1)}, bf16[128,1280]{1,0:T(8,128)(2,1)}, u32[]{:S(2)}) copy-start(bf16[128,1280]{1,0:T(8,128)(2,1)} %copy-done.15) | copy-start | bytes 983044
  119.0 16.4 %all-to-all-start.2 = ((bf16[16,80,128]{2,1,0:T(8,128)(2,1)}), bf16[16,80,128]{2,1,0:T(8,128)(2,1)S(1)}, u32[]{:S(2)}, u32[]{:S(2)}) async-start(bf16[16,80,128]{2,1,0:T(8,128)(2,1)} %bitcast.10), calls=%async_computation.2 | async-start | bytes 655360 | tf_op jit(solution)/shard_map/all_to_all | solution.py:187
  124.8 2.1 %collective-permute-start.10 = (f32[2]{0:T(128)S(1)}, f32[2]{0:T(128)S(1)}, u32[]{:S(2)}, u32[]{:S(2)}) collective-permute-start(f32[2]{0:T(128)S(1)} %get-tuple-element.25), channel_id=1, source_target_pairs={{0,64},{64,0},{1,65},{65,1},{2,66},{66,2},{3,67},{67,3},{4,68},{68... | collective-permute-start | bytes 32 | tf_op jit(solution)/shard_map/ppermute | solution.py:20
  126.9 2.7 %collective-permute-start.11 = (f32[2]{0:T(128)S(1)}, f32[2]{0:T(128)S(1)}, u32[]{:S(2)}, u32[]{:S(2)}) collective-permute-start(f32[2]{0:T(128)S(1)} %add.104), channel_id=1, source_target_pairs={{0,128},{128,0},{1,129},{129,1},{2,130},{130,2},{3,131},{131,3},{4... | collective-permute-start | bytes 32 | tf_op jit(solution)/shard_map/ppermute | solution.py:24
  135.4 7.1 %collective-permute-start.9 = (f32[80,128]{1,0:T(8,128)S(1)}, f32[80,128]{1,0:T(8,128)S(1)}, u32[]{:S(2)}, u32[]{:S(2)}) collective-permute-start(f32[80,128]{1,0:T(8,128)S(1)} %convert_reduce_fusion), channel_id=1, source_target_pairs={{0,0},{1,1},{2,64},{3,65},{4,128},{5,129},{6,192},{7,193},{8,2},{9... | collective-permute-start | bytes 122888 | tf_op jit(solution)/shard_map/ppermute | solution.py:47
  142.6 1.2 collective-permute-start.12
  143.8 10.8 %collective-permute-start.13 = (f32[80]{0:T(128)S(1)}, f32[80]{0:T(128)S(1)}, u32[]{:S(2)}, u32[]{:S(2)}) collective-permute-start(f32[80]{0:T(128)S(1)} %add.110), channel_id=1, source_target_pairs={{0,128},{128,0},{1,129},{129,1},{2,130},{130,2},{3,131},{131,3},{4... | collective-permute-start | bytes 968 | tf_op jit(solution)/shard_map/ppermute | solution.py:24
  (6 other events, 4.5 us)

commit v2 on v0

v2 whole, which is shorter than its diff:
```python
import jax
import jax.numpy as jnp
from jax import lax
from jax.experimental import pallas as pl
from jax.experimental.pallas import tpu as pltpu
from jax.sharding import Mesh, PartitionSpec as P

EPSILON = 1e-06
BETA = 1.0
SIZES = {"xl": 2, "co": 2, "z": 8, "y": 4, "xh": 2}
CTX = ("xl", "co")
VOC = ("z", "y", "xh")
F32 = jnp.float32
BF16 = jnp.bfloat16
F16 = jnp.float16
PARAMS = pltpu.CompilerParams(vmem_limit_bytes=48 * 1024 * 1024)
SMEM = pl.BlockSpec(memory_space=pltpu.SMEM)
VMEM = pl.BlockSpec(memory_space=pltpu.VMEM)


def core_swap(x):
    return lax.ppermute(x, "co", [(0, 1), (1, 0)])


def chip_swap(x):
    return lax.ppermute(x, "xl", [(0, 1), (1, 0)])


def both_swap(x):
    return lax.ppermute(x, CTX, [(0, 3), (3, 0), (1, 2), (2, 1)])


def x_ring(x, cross):
    perm = []
    for xl in range(2):
        for co in range(2):
            for xh in range(2):
                to = (2 * xh + xl + (1 if co else -1)) % 4
                core = 1 - co if cross else co
                perm.append(((xl * 2 + co) * 2 + xh, ((to % 2) * 2 + core) * 2 + to // 2))
    return lax.ppermute(x, ("xl", "co", "xh"), perm)


def cost(flops, nbytes):
    return pl.CostEstimate(flops=flops, bytes_accessed=nbytes, transcendentals=0)


def normed_slice(ctx, k, hidden_ref, gain_ref, inv):
    toks, pair, width = hidden_ref.shape
    feats = width // 4
    at = pl.ds(pl.multiple_of((ctx ^ k) * feats, 128), feats)
    wide = hidden_ref[:, :, at].astype(F32).reshape(toks * pair, feats)
    return (wide * inv * gain_ref[:, at].astype(F32)).astype(BF16)


def far_kernel(ctx_ref, hidden_ref, gain_ref, far_ref, far_sib_ref, inv_ref, keep_ref):
    toks, pair, width = hidden_ref.shape
    feats = width // 4
    total = None
    for f in range(4):
        wide = hidden_ref[:, :, f * feats : (f + 1) * feats].astype(F32).reshape(toks * pair, feats)
        part = jnp.sum(wide * wide, axis=-1, keepdims=True)
        total = part if total is None else total + part
    inv = lax.rsqrt(total / width + EPSILON)
    inv_ref[...] = inv
    keep_ref[...] = inv
    far_ref[...] = normed_slice(ctx_ref[0], 2, hidden_ref, gain_ref, inv)
    far_sib_ref[...] = normed_slice(ctx_ref[0], 3, hidden_ref, gain_ref, inv)


def near_kernel(ctx_ref, hidden_ref, gain_ref, inv_ref, own_ref, sib_ref):
    inv = inv_ref[...]
    own_ref[...] = normed_slice(ctx_ref[0], 0, hidden_ref, gain_ref, inv)
    sib_ref[...] = normed_slice(ctx_ref[0], 1, hidden_ref, gain_ref, inv)


def norm_blocks(ctx, hidden, gain):
    toks, pair, width = hidden.shape
    feats = width // 4
    step = 16
    gain = gain.reshape(1, width)
    inv_spec = pl.BlockSpec((step * pair, 1), lambda i: (i, 0))
    shared = [
        SMEM,
        pl.BlockSpec((step, pair, width), lambda i: (i, 0, 0)),
        pl.BlockSpec((1, width), lambda i: (0, 0)),
    ]
    outs = [pl.BlockSpec((step * pair, feats), lambda i: (i, 0))] * 2
    block = jax.ShapeDtypeStruct((toks * pair, feats), BF16)
    far, far_sib, inv, keep = pl.pallas_call(
        far_kernel,
        grid=(toks // step,),
        in_specs=shared,
        out_specs=outs + [inv_spec] * 2,
        out_shape=[block, block]
        + [jax.ShapeDtypeStruct((toks * pair, 1), F32), pltpu.HBM((toks * pair, 1), F32)],
        compiler_params=PARAMS,
    )(ctx.reshape(1), hidden, gain)
    own, sib = pl.pallas_call(
        near_kernel,
        grid=(toks // step,),
        in_specs=shared + [inv_spec],
        out_specs=outs,
        out_shape=[pltpu.HBM((toks * pair, feats), BF16), block],
        compiler_params=PARAMS,
        cost_estimate=cost(0, 4 * hidden.size),
    )(ctx.reshape(1), hidden, gain, inv)
    return own, sib, far, far_sib, keep


def load_kernel(from_ref, to_ref, sem):
    copy = pltpu.make_async_copy(from_ref, to_ref, sem)
    copy.start()
    copy.wait()


def load(x):
    return pl.pallas_call(
        load_kernel,
        in_specs=[pl.BlockSpec(memory_space=pltpu.HBM)],
        out_specs=VMEM,
        out_shape=pltpu.VMEM(x.shape, x.dtype),
        scratch_shapes=[pltpu.SemaphoreType.DMA],
        compiler_params=PARAMS,
        cost_estimate=cost(1 << 32, 2 * x.size),
    )(x)


def softmax_kernel(near_ref, sib_ref, far_ref, target_ref, exp_ref, own_ref, stats_ref):
    logits = near_ref[...] + sib_ref[...] + far_ref[...].astype(F32)
    hit = lax.broadcasted_iota(jnp.int32, logits.shape, 1) == target_ref[...]
    top = jnp.max(logits, axis=-1, keepdims=True)
    below = logits - top
    exps = jnp.exp(below)
    exp_ref[...] = jnp.where(hit, -1.0, exps).T.astype(BF16)
    columns = [
        top,
        jnp.sum(exps, axis=-1, keepdims=True),
        jnp.sum(exps * below, axis=-1, keepdims=True),
        jnp.sum(jnp.where(hit, logits, 0.0), axis=-1, keepdims=True),
    ]
    rows = logits.shape[0]
    lane = lax.broadcasted_iota(jnp.int32, (rows, 128), 1)
    packed = jnp.zeros((rows, 128), F32)
    for i, column in enumerate(columns):
        packed = jnp.where(lane == i, column, packed)
    lines = packed.T[:8]
    own_ref[...] = lines
    stats_ref[...] = jnp.broadcast_to(lines[None], stats_ref.shape)


def softmax_parts(near, sib, far, targets, shards):
    rows, vocab = near.shape
    return pl.pallas_call(
        softmax_kernel,
        out_shape=[
            jax.ShapeDtypeStruct((vocab, rows), BF16),
            jax.ShapeDtypeStruct((8, rows), F32),
            pltpu.HBM((shards, 8, rows), F32),
        ],
        compiler_params=PARAMS,
    )(near, sib, far, targets)


def combine_kernel(first_ref, length_ref, own_ref, shards_ref, out_ref):
    tops, sums, dots, picks = (shards_ref[:, i, :] for i in range(4))
    rows = tops.shape[1]
    tokens = 2 * rows
    top = jnp.max(tops, axis=0, keepdims=True)
    shift = tops - top
    scale = jnp.exp(shift)
    total = jnp.sum(scale * sums, axis=0, keepdims=True)
    dot = jnp.sum(scale * (dots + sums * shift), axis=0, keepdims=True)
    target = jnp.sum(picks, axis=0, keepdims=True)
    log_norm = top + jnp.log(total)
    lane = lax.broadcasted_iota(jnp.int32, (1, rows), 1)
    second = lane % 2 == 1
    length = jnp.where(second, length_ref[1], length_ref[0])
    mask = (first_ref[0] + lane // 2 >= length).astype(F32)
    counts = [(tokens - length_ref[s]).astype(F32) for s in range(2)]
    ratio = jnp.where(second, jnp.full((1, rows), counts[0]) / counts[1], -1.0) * mask
    logp = mask * (target - log_norm)
    lines = [
        ratio * jnp.exp(own_ref[0:1, :] - log_norm),
        ratio * (1.0 - jnp.exp(target - log_norm)),
        jnp.broadcast_to(jnp.sum(jnp.where(second, 0.0, logp), axis=1, keepdims=True), (1, rows)),
        jnp.broadcast_to(jnp.sum(jnp.where(second, logp, 0.0), axis=1, keepdims=True), (1, rows)),
        ratio * (target - top - dot / total),
    ]
    line = lax.broadcasted_iota(jnp.int32, (8, rows), 0)
    packed = jnp.zeros((8, rows), F32)
    for i, value in enumerate(lines):
        packed = jnp.where(line == i, value, packed)
    out_ref[...] = packed


def combine(first, length, own, shards):
    return pl.pallas_call(
        combine_kernel,
        in_specs=[SMEM, SMEM, pl.BlockSpec(own.shape), pl.BlockSpec(shards.shape)],
        out_shape=jax.ShapeDtypeStruct((8, shards.shape[2]), F32),
        compiler_params=PARAMS,
    )(first.reshape(1), length, own, shards)


def gradient(value, line):
    return jnp.where(value < 0.0, line[1:2, :], -line[0:1, :] * value)


def loss_kernel(length_ref, mean_ref, scale_ref, l0, l1, l2, l3, out_ref):
    rows = l0.shape[1]
    sums = (l0[2:4, :] + l1[2:4, :]) + (l2[2:4, :] + l3[2:4, :])
    counts = [
        jnp.full((1, rows), (2 * rows - length_ref[s]).astype(F32)) for s in range(2)
    ]
    means = [sums[s : s + 1, :] / counts[s] for s in range(2)]
    margin = BETA * (means[0] - mean_ref[0] - (means[1] - mean_ref[1]))
    loss = jnp.maximum(-margin, 0.0) + jnp.log1p(jnp.exp(-jnp.abs(margin)))
    weight = scale_ref[0] * BETA / (1.0 + jnp.exp(margin)) / counts[0]
    line = lax.broadcasted_iota(jnp.int32, out_ref.shape, 0)
    out_ref[...] = jnp.where(line == 0, weight, loss)


def loss_lines(length, mean, scale, lines):
    return pl.pallas_call(
        loss_kernel,
        in_specs=[SMEM] * 3 + [VMEM] * 4,
        out_specs=VMEM,
        out_shape=jax.ShapeDtypeStruct(lines[0].shape, F32),
        compiler_params=PARAMS,
    )(length, mean, scale.reshape(1), *lines)


def stage_kernel(e0, e1, e2, e3, out_ref):
    rows = e0.shape[1]
    for k, ref in enumerate((e0, e1, e2, e3)):
        out_ref[:, k * rows : (k + 1) * rows] = ref[...]


def stage(exps):
    vocab, rows = exps[0].shape
    return pl.pallas_call(
        stage_kernel,
        in_specs=[VMEM] * 4,
        out_specs=VMEM,
        out_shape=pltpu.VMEM((vocab, 4 * rows), BF16),
        compiler_params=PARAMS,
        cost_estimate=cost(0, 16 * vocab * rows),
    )(*exps)


def back_kernel(ctx_ref, head_ref, exps, l0, l1, l2, l3, out_ref, grads):
    rows = l0.shape[1]
    share = out_ref.shape[4]

    @pl.when(pl.program_id(0) == 0)
    def _():
        for k, line in enumerate((l0, l1, l2, l3)):
            at = slice(k * rows, (k + 1) * rows)
            grads[:, at] = gradient(exps[:, at].astype(F32), line).astype(BF16)

    half = pl.ds(pl.multiple_of(pl.program_id(0) * 8 * share, 8 * share), 8 * share)
    acc = jnp.dot(head_ref[half, :], grads[...], preferred_element_type=F32).astype(BF16)
    for k in range(4):
        for y in range(4):
            for b in range(2):
                at = (2 * y + b) * share
                out_ref[ctx_ref[0] ^ k, y, b, 0] = acc[
                    at : at + share, k * rows : (k + 1) * rows
                ]


def back_blocks(ctx, head, exps, lines):
    feats, vocab = head.shape
    rows = lines[0].shape[1]
    share = feats // 16
    return pl.pallas_call(
        back_kernel,
        grid=(2,),
        in_specs=[SMEM] + [VMEM] * 6,
        out_specs=pl.BlockSpec((4, 4, 2, 1, share, rows), lambda i: (0, 0, 0, i, 0, 0)),
        out_shape=pltpu.HBM((4, 4, 2, 2, share, rows), BF16),
        scratch_shapes=[pltpu.VMEM((vocab, 4 * rows), BF16)],
        compiler_params=PARAMS,
        cost_estimate=cost(8 * feats * vocab * rows, 4 * feats * vocab),
    )(ctx.reshape(1), head, exps, *lines)


def sum_kernel(in_ref, out_ref):
    out_ref[0] = jnp.sum(in_ref[0].astype(F32), axis=0).astype(BF16)


def sum_sources(x):
    outer, inner, rest = x.shape[0], x.shape[1], x.shape[2:]
    zeros = (0,) * len(rest)
    return pl.pallas_call(
        sum_kernel,
        grid=(outer,),
        in_specs=[pl.BlockSpec((1, inner) + rest, lambda i: (i, 0) + zeros)],
        out_specs=pl.BlockSpec((1,) + rest, lambda i: (i,) + zeros),
        out_shape=pltpu.HBM((outer,) + rest, BF16),
        compiler_params=PARAMS,
    )(x)


def head_kernel(w_ref, n0, n1, n2, n3, e0, e1, e2, e3, l0, l1, l2, l3, out_ref, grads):
    rows = e0.shape[1]

    @pl.when(pl.program_id(0) == 0)
    def _():
        for k, (exp_ref, line) in enumerate(zip((e0, e1, e2, e3), (l0, l1, l2, l3))):
            grad = gradient(exp_ref[...].astype(F32), line)
            grads[k * rows : (k + 1) * rows, :] = grad.T.astype(BF16)

    n = jnp.concatenate([n0[...], n1[...], n2[...], n3[...]], axis=0)
    acc = lax.dot_general(n, grads[...], (((0,), (0,)), ((), ())), preferred_element_type=F32)
    out_ref[...] = (w_ref[0:1, 0:1] * acc).astype(BF16)


def head_blocks(weight, ns, exps, lines):
    rows, feats = ns[0].shape
    vocab = exps[0].shape[0]
    block = 256
    return pl.pallas_call(
        head_kernel,
        grid=(feats // block,),
        in_specs=[VMEM]
        + [pl.BlockSpec((rows, block), lambda i: (0, i))] * 4
        + [VMEM] * 8,
        out_specs=pl.BlockSpec((block, vocab), lambda i: (i, 0)),
        out_shape=jax.ShapeDtypeStruct((feats, vocab), BF16),
        scratch_shapes=[pltpu.VMEM((4 * rows, vocab), BF16)],
        compiler_params=PARAMS,
        cost_estimate=cost(8 * feats * vocab * rows, 4 * feats * vocab),
    )(weight, *ns, *exps, *lines)


def on_device(hidden, gain, head, targets, prompt_length, reference_mean, loss_scale):
    tok_dev, seq_pair, model_width = hidden.shape
    feats, vocab_dev = head.shape
    rows = tok_dev * seq_pair
    ctx = lax.axis_index(CTX)
    voc = lax.axis_index(VOC)

    n_own, to_sib, to_far, to_far_sib, inv_rms = norm_blocks(ctx, hidden, gain)
    n_far_sib = x_ring(to_far_sib, True)
    n_far = x_ring(to_far, False)
    n_sib = core_swap(to_sib)
    head_near = load(head)

    def logits_of(n):
        return jnp.dot(n, head_near, preferred_element_type=F32)

    n_far, n_far_sib, sib = lax.optimization_barrier((n_far, n_far_sib, logits_of(n_sib)))
    ns = (n_own, n_sib, n_far, n_far_sib)
    far_sib = core_swap(logits_of(n_far_sib).astype(F16))
    far = lax.optimization_barrier(logits_of(n_far))
    far = chip_swap((far + far_sib.astype(F32)).astype(F16))
    local_target = targets.reshape(rows, 1) - voc * vocab_dev
    exps, own, stats = softmax_parts(logits_of(n_own), core_swap(sib), far.astype(F32), local_target, 64)
    shards = lax.all_to_all(stats, VOC, 0, 0)
    e_far = chip_swap(exps)
    e_sib = core_swap(exps)
    e_far_sib = core_swap(e_far)

    every_exp = (exps, e_sib, e_far, e_far_sib)

    own_lines = combine(ctx * tok_dev, prompt_length, own, shards)
    lines = (own_lines, core_swap(own_lines), chip_swap(own_lines), both_swap(own_lines))
    back = back_blocks(ctx, head_near, stage(every_exp), lines)

    loss = loss_lines(prompt_length, reference_mean, loss_scale, lines)
    dpo_loss = loss[1, 0]

    near_sum = lax.all_to_all(
        back.reshape((32,) + back.shape[3:]), ("xl", "co", "y", "xh"), 0, 0
    )
    head_grad = head_blocks(loss, ns, every_exp, lines)
    near_sum, head_grad = lax.optimization_barrier((near_sum, head_grad))
    near_sum = sum_sources(near_sum.reshape((4, 8) + back.shape[3:]))
    over_z = lax.all_to_all(near_sum.reshape((8,) + back.shape[4:]), "z", 0, 0)
    normed_grad = jnp.sum(over_z.astype(F32), axis=0)

    share = feats // 16
    weight = loss[0]
    normed_grad = normed_grad * weight
    inner_mean = weight * own_lines[4] / model_width
    inv_row = inv_rms.reshape(rows)
    gain_own = lax.dynamic_slice_in_dim(gain, voc * share, share, 0).astype(F32)
    mine = lax.dynamic_slice_in_dim(hidden, voc * share, share, 2)
    unit = mine.reshape(rows, share).T.astype(F32) * inv_row
    hidden_grad = (inv_row * (normed_grad * gain_own[:, None] - unit * inner_mean)).astype(BF16)
    hidden_grad = hidden_grad.T.reshape(tok_dev, seq_pair, share)
    gain_grad = jnp.sum(normed_grad * unit, axis=1)
    gain_grad = (gain_grad + core_swap(gain_grad)) + (chip_swap(gain_grad) + both_swap(gain_grad))
    return (hidden_grad, gain_grad, head_grad, dpo_loss)


def solution(mesh):
    fine = Mesh(mesh.devices.reshape(tuple(SIZES.values())), tuple(SIZES))
    in_specs = (P(CTX, None, None), P(), P(CTX, VOC), P(CTX, None), P(), P(), P())
    out_specs = (P(CTX, None, VOC), P(VOC), P(CTX, VOC), P())
    return jax.shard_map(
        on_device, mesh=fine, in_specs=in_specs, out_specs=out_specs, check_vma=False
    )
```

time: 1340 us -> 114 us (0.09)
  waiting for transfers between devices: 743 us -> 38.5 us
  blocking collectives: 396 us -> 0 us
  other arithmetic: 72.2 us -> 2.41 us
  local copies, waits for them, and re-layouts: 43.5 us -> 5.46 us
  Pallas kernels: 0 us -> 21.5 us
  between operations: 18.4 us -> 1.56 us
    psum x1 -> x0, waiting for transfers between devices: 660 us -> none  [on_device(): summed = lax.psum(grad_cube, 'vocab')]
    psum x3 -> x0, blocking collectives: 216 us -> none  [the longest x1 149 us: on_device(): lax.psum((jnp.sum(jnp.exp(logits - row_top[:, None]), axis=-1), target_pi...]
    pmax x1 -> x0, blocking collectives: 156 us -> none  [on_device(): row_top = lax.pmax(jnp.max(logits, axis=-1), 'vocab')]
    reduce_sum x4 -> x2, other arithmetic: 52.1 us -> 0.13 us  [the longest x1 0.11 us: on_device(): gain_grad = jnp.sum(normed_grad * unit, axis=1)]
    reduce_scatter x1 -> x0, waiting for transfers between devices: 35.5 us -> none  [on_device(): lax.psum_scatter(jnp.dot(row_block, head, preferred_element_type=jnp.floa...]
    all_to_all x1 -> x3, starting transfers between devices: 50.5 us -> 22.4 us  [the longest x1 14.6 us: on_device(): shards = lax.all_to_all(stats, VOC, 0, 0)]
    all_to_all x1 -> x0, blocking collectives: 23.8 us -> none  [on_device(): lax.all_to_all(normed, 'ctx', split_axis=2, concat_axis=0, tiled=True)]
    all_gather x1 -> x0, waiting for transfers between devices: 22.2 us -> none  [on_device(): shard_rows = lax.all_gather(logit_grad, 'ctx', axis=0, tiled=True)]
  transfers between devices with their start and end apart: 4 -> 18, of which waited for: 4 -> 7; matrix products, arithmetic and copies ran while one was open for 0% -> 7% of each run, Pallas kernels for 0% -> 12%
where the time goes in v2:
time: 114 us; the launch traced here: 113 us
  starting transfers between devices  38.6 us (34%)
  waiting for transfers between devices  38.5 us (34%)
  Pallas kernels  21.5 us (19%)
  local copies, waits for them, and re-layouts  5.46 us (5%)
  matrix products  5.39 us (5%)
  other arithmetic  2.41 us (2%)
  between operations  1.56 us (1%)
    all_to_all x1, starting transfers between devices, on_device(): shards = lax.all_to_all(stats, VOC, 0, 0)  14.6 us
    all_to_all x1, waiting for transfers between devices, on_device(): shards = lax.all_to_all(stats, VOC, 0, 0)  10.6 us
    all_to_all x1, waiting for transfers between devices, on_device(): lax.all_to_all(back.reshape((32,) + back.shape[3:]), ('xl', 'co', 'y', 'x...  9.81 us
    ppermute x4, waiting for transfers between devices, chip_swap(): return lax.ppermute(x, 'xl', [(0, 1), (1, 0)])  8.78 us
    pallas_call x1, Pallas kernels, head_blocks(): pl.pallas_call(head_kernel, grid=(feats // block,), in_specs=[VMEM] + [pl...  6.75 us
    all_to_all x1, waiting for transfers between devices, on_device(): over_z = lax.all_to_all(near_sum.reshape((8,) + back.shape[4:]), 'z', 0, 0)  6.7 us
    ppermute x2, starting transfers between devices, both_swap(): return lax.ppermute(x, CTX, [(0, 3), (3, 0), (1, 2), (2, 1)])  5.39 us
    dot_general x4, matrix products, logits_of(): return jnp.dot(n, head_near, preferred_element_type=F32)  5.39 us
  transfers between devices with their start and end apart: 18, of which 7 were waited for; matrix products, arithmetic and copies ran while one was open for 7% of the time, Pallas kernels for 12%

profile of v2, /device:TPU:1, one launch (start us, length us, event | category | flops | bytes accessed | tf_op | source)
XLA Modules:
  0.0 113.4 jit_solution(9598300641213046465)
XLA Ops:
  0.6 0.7 reshape.57.gain_ref
  1.4 1.3 %copy-done = bf16[64,2,5120]{2,1,0:T(2,128)(2,1)S(1)} copy-done((bf16[64,2,5120]{2,1,0:T(2,128)(2,1)S(1)}, bf16[64,2,5120]{2,1,0:T(2,128)(2,1)}, u32[]{:S(2)}) %copy-start) | copy-done | bytes 1310744
  2.7 2.2 %shard_map.102 = (bf16[128,1280]{1,0:T(8,128)(2,1)}, bf16[128,1280]{1,0:T(8,128)(2,1)}, f32[128,1]{1,0:T(8,128)S(1)}, f32[128,1]{1,0:T(8,128)}) custom-call(s32[1]{0:T(128)} %bitcast.ctx_ref, bf16[64,2,5120]{2,1,0:T(2,128)(2,1)S(1)} %copy-done, bf16[1,5120]{1,0:T(2,128)(2,1)S(1)} %reshape.57.gain_ref), custom_call_target="tpu_custom_call" | custom-call | tf_op jit(solution)/shard_map/pallas_call | solution.py:90
  4.9 2.0 %collective-permute-start = (bf16[128,1280]{1,0:T(8,128)(2,1)}, bf16[128,1280]{1,0:T(8,128)(2,1)}, u32[]{:S(2)}, u32[]{:S(2)}) collective-permute-start(bf16[128,1280]{1,0:T(8,128)(2,1)} %get-tuple-element.21), channel_id=1, source_target_pairs={{0,129},{1,128},{64,192},{65,193},{128,0},{129,1},{192,65},{193,64... | collective-permute-start | bytes 983048 | tf_op jit(solution)/shard_map/ppermute | solution.py:41
  6.9 2.8 %collective-permute-start.1 = (bf16[128,1280]{1,0:T(8,128)(2,1)}, bf16[128,1280]{1,0:T(8,128)(2,1)}, u32[]{:S(2)}, u32[]{:S(2)}) collective-permute-start(bf16[128,1280]{1,0:T(8,128)(2,1)} %get-tuple-element.22), channel_id=1, source_target_pairs={{0,193},{1,192},{64,128},{65,129},{128,64},{129,65},{192,1},{193,0... | collective-permute-start | bytes 983048 | tf_op jit(solution)/shard_map/ppermute | solution.py:41
  9.7 1.8 %shard_map.104 = (bf16[128,1280]{1,0:T(8,128)(2,1)}, bf16[128,1280]{1,0:T(8,128)(2,1)}) custom-call(s32[1]{0:T(128)} %bitcast.ctx_ref, bf16[64,2,5120]{2,1,0:T(2,128)(2,1)S(1)} %copy-done, bf16[1,5120]{1,0:T(2,128)(2,1)S(1)} %reshape.57.gain_ref, f32[128,1]{1,0:T(8,128)S(1)} %get-tuple-element.19.inv_ref), custom_call_target="tpu_custom_call" | custom-call | bytes 2621440 | tf_op jit(solution)/shard_map/pallas_call | solution.py:99
  12.3 1.9 %shard_map.103.head_ref = bf16[1280,1280]{1,0:T(8,128)(2,1)S(1)} custom-call(bf16[1280,1280]{1,0:T(8,128)(2,1)} %from_ref.1), custom_call_target="tpu_custom_call" | custom-call | flops 4294967296 | bytes 3276800 | tf_op jit(solution)/shard_map/pallas_call | solution.py:118
  14.3 1.6 %fusion.4 = f32[128,1280]{1,0:T(8,128)S(1)} fusion(bf16[128,1280]{1,0:T(8,128)(2,1)} %collective-permute-done.2.n1, bf16[1280,1280]{1,0:T(8,128)(2,1)S(1)} %shard_map.103.head_ref), kind=kOutput, calls=%fused_computation.15 | convolution fusion | flops 419430400 | bytes 4259840 | tf_op jit(solution)/shard_map/dot_general | solution.py:352
  15.9 2.4 %collective-permute-done.1.n3 = bf16[128,1280]{1,0:T(8,128)(2,1)} collective-permute-done((bf16[128,1280]{1,0:T(8,128)(2,1)}, bf16[128,1280]{1,0:T(8,128)(2,1)}, u32[]{:S(2)}, u32[]{:S(2)}) %collective-permute-start.1) | collective-permute-done | bytes 327712 | tf_op jit(solution)/shard_map/ppermute | solution.py:41
  18.3 1.6 %convolution_convert_fusion = f16[128,1280]{1,0:T(8,128)(2,1)S(1)} fusion(bf16[128,1280]{1,0:T(8,128)(2,1)} %collective-permute-done.1.n3, bf16[1280,1280]{1,0:T(8,128)(2,1)S(1)} %shard_map.103.head_ref), kind=kOutput, calls=%fused_computation | convolution fusion | flops 419594240 | bytes 3932160 | tf_op jit(solution)/shard_map/dot_general | solution.py:352
  20.0 1.6 %fusion.5 = f32[128,1280]{1,0:T(8,128)S(1)} fusion(bf16[128,1280]{1,0:T(8,128)(2,1)} %collective-permute-done.n2, bf16[1280,1280]{1,0:T(8,128)(2,1)S(1)} %shard_map.103.head_ref), kind=kOutput, calls=%fused_computation.16 | convolution fusion | flops 419430400 | bytes 4259840 | tf_op jit(solution)/shard_map/dot_general | solution.py:352
  23.0 8.7 %collective-permute-done.5 = f16[128,1280]{1,0:T(8,128)(2,1)S(1)} collective-permute-done((f16[128,1280]{1,0:T(8,128)(2,1)S(1)}, f16[128,1280]{1,0:T(8,128)(2,1)S(1)}, u32[]{:S(2)}, u32[]{:S(2)}) %collective-permute-start.5) | collective-permute-done | bytes 327712 | tf_op jit(solution)/shard_map/ppermute | solution.py:26
  31.7 1.3 %shard_map.105 = (bf16[1280,128]{1,0:T(8,128)(2,1)}, f32[8,128]{1,0:T(8,128)S(1)}, f32[64,8,128]{2,1,0:T(8,128)}) custom-call(f32[128,1280]{1,0:T(8,128)S(1)} %fusion.3.near_ref, f32[128,1280]{1,0:T(8,128)S(1)} %collective-permute-done.3.sib_ref, f32[128,1280]{1,0:T(8,128)S(1)} %convert_element_type.34.far_ref, s32[128,1]{1,0:T(8,128)S(1)} %sub.16.target_ref), custom_call_target="tpu_custom_call" | custom-call | tf_op jit(solution)/shard_map/pallas_call | solution.py:154
  33.1 14.6 %all-to-all-start = ((f32[64,8,128]{2,1,0:T(8,128)}), f32[64,8,128]{2,1,0:T(8,128)S(1)}, u32[]{:S(2)}, u32[]{:S(2)}) async-start(f32[64,8,128]{2,1,0:T(8,128)} %get-tuple-element.29), calls=%async_computation | async-start | bytes 524288 | tf_op jit(solution)/shard_map/all_to_all | solution.py:361
  47.7 1.5 %collective-permute-start.6 = (bf16[1280,128]{1,0:T(8,128)(2,1)}, bf16[1280,128]{1,0:T(8,128)(2,1)}, u32[]{:S(2)}, u32[]{:S(2)}) collective-permute-start(bf16[1280,128]{1,0:T(8,128)(2,1)} %get-tuple-element.27.e0), channel_id=1, source_target_pairs={{0,64},{64,0},{1,65},{65,1},{2,66},{66,2},{3,67},{67,3},{4,68},{68... | collective-permute-start | bytes 983048 | tf_op jit(solution)/shard_map/ppermute | solution.py:22
  49.3 10.6 %all-to-all-done.shards_ref = f32[64,8,128]{2,1,0:T(8,128)S(1)} async-done(((f32[64,8,128]{2,1,0:T(8,128)}), f32[64,8,128]{2,1,0:T(8,128)S(1)}, u32[]{:S(2)}, u32[]{:S(2)}) %all-to-all-start) | async-done | bytes 262176 | tf_op jit(solution)/shard_map/all_to_all | solution.py:361
  60.6 2.8 %collective-permute-start.11 = (f32[8,128]{1,0:T(8,128)S(1)}, f32[8,128]{1,0:T(8,128)S(1)}, u32[]{:S(2)}, u32[]{:S(2)}) collective-permute-start(f32[8,128]{1,0:T(8,128)S(1)} %shard_map.107.l0), channel_id=1, source_target_pairs={{0,192},{192,0},{64,128},{128,64},{1,193},{193,1},{65,129},{129,65... | collective-permute-start | bytes 12296 | tf_op jit(solution)/shard_map/ppermute | solution.py:30
  63.4 2.0 %collective-permute-start.10 = (f32[8,128]{1,0:T(8,128)S(1)}, f32[8,128]{1,0:T(8,128)S(1)}, u32[]{:S(2)}, u32[]{:S(2)}) collective-permute-start(f32[8,128]{1,0:T(8,128)S(1)} %shard_map.107.l0), channel_id=1, source_target_pairs={{0,128},{128,0},{1,129},{129,1},{2,130},{130,2},{3,131},{131,3},{4... | collective-permute-start | bytes 12296 | tf_op jit(solution)/shard_map/ppermute | solution.py:26
  65.4 1.5 %shard_map.106.exps = bf16[1280,512]{1,0:T(8,128)(2,1)S(1)} custom-call(bf16[1280,128]{1,0:T(8,128)(2,1)} %get-tuple-element.27.e0, bf16[1280,128]{1,0:T(8,128)(2,1)} %collective-permute-done.6.e1, bf16[1280,128]{1,0:T(8,128)(2,1)} %collective-permute-done.7.e2, bf16[1280,128]{1,0:T(8,128)(2,1)} %collective-permute-done.8.e3), custom_call_target="tpu_custom_call" | custom-call | bytes 2621440 | tf_op jit(solution)/shard_map/pallas_call | solution.py:242
  66.9 3.5 %shard_map.108 = bf16[4,4,2,2,80,128]{5,4,3,2,1,0:T(8,128)(2,1)} custom-call(s32[1]{0:T(128)} %bitcast.ctx_ref, bf16[1280,1280]{1,0:T(8,128)(2,1)S(1)} %shard_map.103.head_ref, bf16[1280,512]{1,0:T(8,128)(2,1)S(1)} %shard_map.106.exps, f32[8,128]{1,0:T(8,128)S(1)} %shard_map.107.l0, f32[8,128]{1,0:T(8,128)S(1)} %collective-permute-done.9.l1, ...), custom_call_target="tpu_custom_call" | custom-call | flops 1677721600 | bytes 6553600 | tf_op jit(solution)/shard_map/pallas_call | solution.py:277
  70.4 4.4 %all-to-all-start.1 = ((bf16[32,2,80,128]{3,2,1,0:T(8,128)(2,1)}), bf16[32,2,80,128]{3,2,1,0:T(8,128)(2,1)S(1)}, u32[]{:S(2)}, u32[]{:S(2)}) async-start(bf16[32,2,80,128]{3,2,1,0:T(8,128)(2,1)} %bitcast.34), calls=%async_computation.1 | async-start | bytes 2621440 | tf_op jit(solution)/shard_map/all_to_all | solution.py:375
  75.4 1.0 constant_dynamic-slice_fusion
  77.2 1.0 copy-done.2
  78.2 6.8 %shard_map.110 = bf16[1280,1280]{1,0:T(8,128)(2,1)} custom-call(f32[8,128]{1,0:T(8,128)S(1)} %shard_map.109.w_ref, bf16[128,1280]{1,0:T(8,128)(2,1)S(1)} %copy-done.2, bf16[128,1280]{1,0:T(8,128)(2,1)} %collective-permute-done.2.n1, bf16[128,1280]{1,0:T(8,128)(2,1)} %collective-permute-done.n2, bf16[128,1280]{1,0:T(8,128)(2,1)} %collective-permute-done.1.n3, ...), custom_call_target="tpu_custom_call" | custom-call | flops 1677721600 | bytes 6553600 | tf_op jit(solution)/shard_map/pallas_call | solution.py:324
  84.9 9.8 %all-to-all-done.1 = bf16[32,2,80,128]{3,2,1,0:T(8,128)(2,1)S(1)} async-done(((bf16[32,2,80,128]{3,2,1,0:T(8,128)(2,1)}), bf16[32,2,80,128]{3,2,1,0:T(8,128)(2,1)S(1)}, u32[]{:S(2)}, u32[]{:S(2)}) %all-to-all-start.1) | async-done | bytes 1310752 | tf_op jit(solution)/shard_map/all_to_all | solution.py:375
  94.7 1.4 %shard_map.111 = bf16[4,2,80,128]{3,2,1,0:T(8,128)(2,1)} custom-call(bf16[4,8,2,80,128]{4,3,2,1,0:T(8,128)(2,1)S(1)} %bitcast.33), custom_call_target="tpu_custom_call" | custom-call | tf_op jit(solution)/shard_map/pallas_call | solution.py:296
  96.1 3.4 %all-to-all-start.2 = ((bf16[8,80,128]{2,1,0:T(8,128)(2,1)}), bf16[8,80,128]{2,1,0:T(8,128)(2,1)S(1)}, u32[]{:S(2)}, u32[]{:S(2)}) async-start(bf16[8,80,128]{2,1,0:T(8,128)(2,1)} %bitcast.35), calls=%async_computation.2 | async-start | bytes 327680 | tf_op jit(solution)/shard_map/all_to_all | solution.py:381
  99.5 0.8 dynamic-slice_convert_fusion
  100.8 6.7 %all-to-all-done.2 = bf16[8,80,128]{2,1,0:T(8,128)(2,1)S(1)} async-done(((bf16[8,80,128]{2,1,0:T(8,128)(2,1)}), bf16[8,80,128]{2,1,0:T(8,128)(2,1)S(1)}, u32[]{:S(2)}, u32[]{:S(2)}) %all-to-all-start.2) | async-done | bytes 163872 | tf_op jit(solution)/shard_map/all_to_all | solution.py:381
  107.6 2.5 %collective-permute-start.14 = (f32[80]{0:T(128)S(1)}, f32[80]{0:T(128)S(1)}, u32[]{:S(2)}, u32[]{:S(2)}) collective-permute-start(f32[80]{0:T(128)S(1)} %fusion), channel_id=1, source_target_pairs={{0,192},{192,0},{64,128},{128,64},{1,193},{193,1},{65,129},{129,65... | collective-permute-start | bytes 968 | tf_op jit(solution)/shard_map/ppermute | solution.py:30
  110.2 1.5 %collective-permute-start.13 = (f32[80]{0:T(128)S(1)}, f32[80]{0:T(128)S(1)}, u32[]{:S(2)}, u32[]{:S(2)}) collective-permute-start(f32[80]{0:T(128)S(1)} %fusion), channel_id=1, source_target_pairs={{0,128},{128,0},{1,129},{129,1},{2,130},{130,2},{3,131},{131,3},{4... | collective-permute-start | bytes 968 | tf_op jit(solution)/shard_map/ppermute | solution.py:26
  111.8 0.7 copy.22
  (47 shorter events, 5.7 us)
Async XLA Ops:
  1.4 1.3 %copy-start = (bf16[64,2,5120]{2,1,0:T(2,128)(2,1)S(1)}, bf16[64,2,5120]{2,1,0:T(2,128)(2,1)}, u32[]{:S(2)}) copy-start(bf16[64,2,5120]{2,1,0:T(2,128)(2,1)} %hidden_ref.3) | copy-start | bytes 3932164
  4.9 11.0 %collective-permute-start = (bf16[128,1280]{1,0:T(8,128)(2,1)}, bf16[128,1280]{1,0:T(8,128)(2,1)}, u32[]{:S(2)}, u32[]{:S(2)}) collective-permute-start(bf16[128,1280]{1,0:T(8,128)(2,1)} %get-tuple-element.21), channel_id=1, source_target_pairs={{0,129},{1,128},{64,192},{65,193},{128,0},{129,1},{192,65},{193,64... | collective-permute-start | bytes 983048 | tf_op jit(solution)/shard_map/ppermute | solution.py:41
  6.9 11.4 %collective-permute-start.1 = (bf16[128,1280]{1,0:T(8,128)(2,1)}, bf16[128,1280]{1,0:T(8,128)(2,1)}, u32[]{:S(2)}, u32[]{:S(2)}) collective-permute-start(bf16[128,1280]{1,0:T(8,128)(2,1)} %get-tuple-element.22), channel_id=1, source_target_pairs={{0,193},{1,192},{64,128},{65,129},{128,64},{129,65},{192,1},{193,0... | collective-permute-start | bytes 983048 | tf_op jit(solution)/shard_map/ppermute | solution.py:41
  11.5 2.8 %collective-permute-start.2 = (bf16[128,1280]{1,0:T(8,128)(2,1)}, bf16[128,1280]{1,0:T(8,128)(2,1)}, u32[]{:S(2)}, u32[]{:S(2)}) collective-permute-start(bf16[128,1280]{1,0:T(8,128)(2,1)} %get-tuple-element.23), channel_id=1, source_target_pairs={{0,64},{64,0},{1,65},{65,1},{2,66},{66,2},{3,67},{67,3},{4,68},{68... | collective-permute-start | bytes 983048 | tf_op jit(solution)/shard_map/ppermute | solution.py:22
  19.9 2.5 %copy-start.1 = (bf16[128,1280]{1,0:T(8,128)(2,1)S(1)}, bf16[128,1280]{1,0:T(8,128)(2,1)}, u32[]{:S(2)}) copy-start(bf16[128,1280]{1,0:T(8,128)(2,1)} %get-tuple-element.20.n0) | copy-start | bytes 983044
  19.9 2.3 %collective-permute-start.4 = (f16[128,1280]{1,0:T(8,128)(2,1)S(1)}, f16[128,1280]{1,0:T(8,128)(2,1)S(1)}, u32[]{:S(2)}, u32[]{:S(2)}) collective-permute-start(f16[128,1280]{1,0:T(8,128)(2,1)S(1)} %convolution_convert_fusion), channel_id=1, source_target_pairs={{0,64},{64,0},{1,65},{65,1},{2,66},{66,2},{3,67},{67,3},{4,68},{68... | collective-permute-start | bytes 983048 | tf_op jit(solution)/shard_map/ppermute | solution.py:22
  21.6 10.1 %collective-permute-start.3 = (f32[128,1280]{1,0:T(8,128)S(1)}, f32[128,1280]{1,0:T(8,128)S(1)}, u32[]{:S(2)}, u32[]{:S(2)}) collective-permute-start(f32[128,1280]{1,0:T(8,128)S(1)} %fusion.4), channel_id=1, source_target_pairs={{0,64},{64,0},{1,65},{65,1},{2,66},{66,2},{3,67},{67,3},{4,68},{68... | collective-permute-start | bytes 1966088 | tf_op jit(solution)/shard_map/ppermute | solution.py:22
  22.3 9.4 %collective-permute-start.5 = (f16[128,1280]{1,0:T(8,128)(2,1)S(1)}, f16[128,1280]{1,0:T(8,128)(2,1)S(1)}, u32[]{:S(2)}, u32[]{:S(2)}) collective-permute-start(f16[128,1280]{1,0:T(8,128)(2,1)S(1)} %add_convert_fusion), channel_id=1, source_target_pairs={{0,128},{128,0},{1,129},{129,1},{2,130},{130,2},{3,131},{131,3},{4... | collective-permute-start | bytes 983048 | tf_op jit(solution)/shard_map/ppermute | solution.py:26
  22.4 37.5 %copy-start.3 = (s32[2]{0:T(128)S(1)}, s32[2]{0:T(128)}, u32[]{:S(2)}) copy-start(s32[2]{0:T(128)} %length_ref.3) | copy-start | bytes 28
  33.0 16.1 %collective-permute-start.7 = (bf16[1280,128]{1,0:T(8,128)(2,1)}, bf16[1280,128]{1,0:T(8,128)(2,1)}, u32[]{:S(2)}, u32[]{:S(2)}) collective-permute-start(bf16[1280,128]{1,0:T(8,128)(2,1)} %get-tuple-element.27.e0), channel_id=1, source_target_pairs={{0,128},{128,0},{1,129},{129,1},{2,130},{130,2},{3,131},{131,3},{4... | collective-permute-start | bytes 983048 | tf_op jit(solution)/shard_map/ppermute | solution.py:26
  33.1 26.7 %all-to-all-start = ((f32[64,8,128]{2,1,0:T(8,128)}), f32[64,8,128]{2,1,0:T(8,128)S(1)}, u32[]{:S(2)}, u32[]{:S(2)}) async-start(f32[64,8,128]{2,1,0:T(8,128)} %get-tuple-element.29), calls=%async_computation | async-start | bytes 524288 | tf_op jit(solution)/shard_map/all_to_all | solution.py:361
  47.7 17.6 %collective-permute-start.6 = (bf16[1280,128]{1,0:T(8,128)(2,1)}, bf16[1280,128]{1,0:T(8,128)(2,1)}, u32[]{:S(2)}, u32[]{:S(2)}) collective-permute-start(bf16[1280,128]{1,0:T(8,128)(2,1)} %get-tuple-element.27.e0), channel_id=1, source_target_pairs={{0,64},{64,0},{1,65},{65,1},{2,66},{66,2},{3,67},{67,3},{4,68},{68... | collective-permute-start | bytes 983048 | tf_op jit(solution)/shard_map/ppermute | solution.py:22
  49.2 16.2 %collective-permute-start.8 = (bf16[1280,128]{1,0:T(8,128)(2,1)}, bf16[1280,128]{1,0:T(8,128)(2,1)}, u32[]{:S(2)}, u32[]{:S(2)}) collective-permute-start(bf16[1280,128]{1,0:T(8,128)(2,1)} %collective-permute-done.7.e2), channel_id=1, source_target_pairs={{0,64},{64,0},{1,65},{65,1},{2,66},{66,2},{3,67},{67,3},{4,68},{68... | collective-permute-start | bytes 983048 | tf_op jit(solution)/shard_map/ppermute | solution.py:22
  60.6 6.3 %collective-permute-start.11 = (f32[8,128]{1,0:T(8,128)S(1)}, f32[8,128]{1,0:T(8,128)S(1)}, u32[]{:S(2)}, u32[]{:S(2)}) collective-permute-start(f32[8,128]{1,0:T(8,128)S(1)} %shard_map.107.l0), channel_id=1, source_target_pairs={{0,192},{192,0},{64,128},{128,64},{1,193},{193,1},{65,129},{129,65... | collective-permute-start | bytes 12296 | tf_op jit(solution)/shard_map/ppermute | solution.py:30
  63.4 3.5 %collective-permute-start.10 = (f32[8,128]{1,0:T(8,128)S(1)}, f32[8,128]{1,0:T(8,128)S(1)}, u32[]{:S(2)}, u32[]{:S(2)}) collective-permute-start(f32[8,128]{1,0:T(8,128)S(1)} %shard_map.107.l0), channel_id=1, source_target_pairs={{0,128},{128,0},{1,129},{129,1},{2,130},{130,2},{3,131},{131,3},{4... | collective-permute-start | bytes 12296 | tf_op jit(solution)/shard_map/ppermute | solution.py:26
  65.4 1.6 %collective-permute-start.9 = (f32[8,128]{1,0:T(8,128)S(1)}, f32[8,128]{1,0:T(8,128)S(1)}, u32[]{:S(2)}, u32[]{:S(2)}) collective-permute-start(f32[8,128]{1,0:T(8,128)S(1)} %shard_map.107.l0), channel_id=1, source_target_pairs={{0,64},{64,0},{1,65},{65,1},{2,66},{66,2},{3,67},{67,3},{4,68},{68... | collective-permute-start | bytes 12296 | tf_op jit(solution)/shard_map/ppermute | solution.py:22
  66.9 9.6 %copy-start.5 = (f32[128,1]{1,0:T(8,128)S(1)}, f32[128,1]{1,0:T(8,128)}, u32[]{:S(2)}) copy-start(f32[128,1]{1,0:T(8,128)} %get-tuple-element.18) | copy-start | bytes 1540
  66.9 9.7 %copy-start.4 = (f32[2]{0:T(128)S(1)}, f32[2]{0:T(128)}, u32[]{:S(2)}) copy-start(f32[2]{0:T(128)} %mean_ref.1) | copy-start | bytes 28
  70.4 24.4 %all-to-all-start.1 = ((bf16[32,2,80,128]{3,2,1,0:T(8,128)(2,1)}), bf16[32,2,80,128]{3,2,1,0:T(8,128)(2,1)S(1)}, u32[]{:S(2)}, u32[]{:S(2)}) async-start(bf16[32,2,80,128]{3,2,1,0:T(8,128)(2,1)} %bitcast.34), calls=%async_computation.1 | async-start | bytes 2621440 | tf_op jit(solution)/shard_map/all_to_all | solution.py:375
  77.2 1.0 copy-start.2
  96.1 11.4 %all-to-all-start.2 = ((bf16[8,80,128]{2,1,0:T(8,128)(2,1)}), bf16[8,80,128]{2,1,0:T(8,128)(2,1)S(1)}, u32[]{:S(2)}, u32[]{:S(2)}) async-start(bf16[8,80,128]{2,1,0:T(8,128)(2,1)} %bitcast.35), calls=%async_computation.2 | async-start | bytes 327680 | tf_op jit(solution)/shard_map/all_to_all | solution.py:381
  107.6 4.9 %collective-permute-start.14 = (f32[80]{0:T(128)S(1)}, f32[80]{0:T(128)S(1)}, u32[]{:S(2)}, u32[]{:S(2)}) collective-permute-start(f32[80]{0:T(128)S(1)} %fusion), channel_id=1, source_target_pairs={{0,192},{192,0},{64,128},{128,64},{1,193},{193,1},{65,129},{129,65... | collective-permute-start | bytes 968 | tf_op jit(solution)/shard_map/ppermute | solution.py:30
  110.2 2.5 %collective-permute-start.13 = (f32[80]{0:T(128)S(1)}, f32[80]{0:T(128)S(1)}, u32[]{:S(2)}, u32[]{:S(2)}) collective-permute-start(f32[80]{0:T(128)S(1)} %fusion), channel_id=1, source_target_pairs={{0,128},{128,0},{1,129},{129,1},{2,130},{130,2},{3,131},{131,3},{4... | collective-permute-start | bytes 968 | tf_op jit(solution)/shard_map/ppermute | solution.py:26
  111.7 1.1 collective-permute-start.12
